TPU v7x, 128 devices: a whole 4x4x4 slice. The times are simulated.
128 devices in a mesh: seq: 16 (over x, y), mp: 8 (over z, core).
Axes of the slice: x: 4, y: 4, z: 4, core: 2. Of those that a mesh axis runs over, the one named last changes fastest.
Arguments:
- lengths: int32 [8], replicated, may hold values from 1 to 4096, 8192 in all
- hidden_in: bfloat16 [8192, 8192], P('seq'), may hold values from -30 to 30
- w_bc: bfloat16 [8192, 4096], P('seq', 'mp'), may hold values from -0.00390625 to 0.00390625
- x_in: bfloat16 [8192, 16384], P('seq', 'mp'), may hold values from -6 to 6
- log_decay: float32 [8192, 256], P('seq', 'mp'), may hold values from -2 to 0, as said below
- dy_in: bfloat16 [8192, 16384], P('seq', 'mp'), may hold values from -6 to 6
Outputs:
- y_out: bfloat16 [8192, 16384], P('seq', 'mp')
- grad_x: bfloat16 [8192, 16384], P('seq', 'mp')
- grad_mant: float32 [8192, 4096], P('seq', 'mp')
- grad_exp: float32 [], replicated
Inputs may be any that keep to these rules, and one draw needn't show every extreme that they name: The lengths sum to 8192 and the longest is exactly 4096. `log_decay`: never positive.
All inputs are finite; a program needn't handle non-finite values.
Results may differ from a plain program's by a relative error of at most 0.02.
Values may be sent and summed in bfloat16 or wider, within the bound.
A program may use at most 256 MiB of HBM per device.

v0:
```python
import jax
import jax.numpy as jnp
from jax import lax
from jax.sharding import PartitionSpec as P

HEADS = 256
GROUPS = 8


HIGH = lax.Precision.HIGHEST


def prefix(value, axis, join, neutral, backward):
    count = lax.axis_size(axis)
    place = lax.axis_index(axis)
    ahead = count - 1 - place if backward else place
    gathered = jax.tree.map(
        lambda a, kind: lax.all_gather(a.astype(kind), axis), value, (jnp.bfloat16, jnp.bfloat16)
    )
    state = jax.tree.map(lambda a, e: jnp.zeros_like(a) + jnp.asarray(e, a.dtype), value, neutral)

    def one(step, state):
        source = count - 1 - step if backward else step
        return join(
            state,
            jax.tree.map(
                lambda a, own: lax.dynamic_index_in_dim(a, source, 0, False).astype(own.dtype),
                gathered,
                value,
            ),
        )

    return lax.fori_loop(0, ahead, one, state)


def link_states(earlier, later):
    return (earlier[0] * later[0], later[0][:, :, None, None] * earlier[1] + later[1])


def quantized(incomplete_figure):
    largest = lax.pmax(jnp.max(jnp.abs(incomplete_figure)), ("seq", "mp"))
    exponent = jnp.ceil(jnp.log2(largest))
    return (jnp.floor(incomplete_figure * jnp.exp2(20.0 - exponent) + 0.5), exponent)


def shards(lengths, hidden_in, w_bc, x_in, log_decay, dy_in):
    rows = x_in.shape[0]
    heads = log_decay.shape[1]
    within_cluster = HEADS // GROUPS
    groups = heads // within_cluster
    width = x_in.shape[1] // heads
    nstate = w_bc.shape[1] // (2 * groups)
    first = lax.axis_index("seq") * rows
    starts = jnp.cumsum(lengths) - lengths
    places = jnp.arange(rows, dtype=jnp.int32)
    flags = jnp.any(starts[:, None] == (first + places)[None, :], axis=0)
    count = jnp.cumsum(flags.astype(jnp.int32))
    running_total = jnp.cumsum(log_decay, axis=0).T
    same = (count[:, None] == count[None, :]) & (places[:, None] >= places[None, :])
    weights = jnp.exp(
        jnp.where(same[None], running_total[:, :, None] - running_total[:, None, :], -jnp.inf)
    )
    w_four = weights.reshape(groups, within_cluster, rows, rows)
    entry = (jnp.exp(running_total) * (count == 0)[None, :].astype(jnp.float32)).reshape(
        groups, within_cluster, rows
    )
    ends = w_four[:, :, -1, :]
    decay = entry[:, :, -1]
    proj = jnp.dot(
        hidden_in,
        lax.all_gather(w_bc, "seq", axis=0, tiled=True),
        preferred_element_type=jnp.float32,
    )
    pairs = proj.astype(jnp.bfloat16).reshape(rows, groups, 2, nstate)
    b_mat = pairs[:, :, 0, :]
    c_mat = pairs[:, :, 1, :]
    b_f32 = b_mat.astype(jnp.float32)
    c_f32 = c_mat.astype(jnp.float32)
    x_four = x_in.reshape(rows, groups, within_cluster, width)
    dy_four = dy_in.reshape(rows, groups, within_cluster, width)
    x_f32 = x_four.astype(jnp.float32)
    dy_f32 = dy_four.astype(jnp.float32)
    s_loc = jnp.einsum("ghs,sghp,sgn->ghpn", ends, x_f32, b_f32, precision=HIGH)
    identity = (jnp.ones_like(decay), jnp.zeros_like(s_loc))
    s_in = prefix((decay, s_loc), "seq", link_states, identity, False)[1]
    gram = jnp.einsum("tgn,sgn->gts", c_mat, b_mat, preferred_element_type=jnp.float32)
    mixed = (gram[:, None] * w_four).astype(jnp.bfloat16)
    y_intra = jnp.einsum("ghts,sghp->tghp", mixed, x_four, preferred_element_type=jnp.float32)
    y_carry = entry.transpose(2, 0, 1)[..., None] * jnp.einsum(
        "tgn,ghpn->tghp", c_f32, s_in, precision=HIGH
    )
    y_out = (y_intra + y_carry).astype(jnp.bfloat16).reshape(rows, heads * width)
    s_grad = jnp.einsum("ght,tghp,tgn->ghpn", entry, dy_f32, c_f32, precision=HIGH)
    rsum = prefix((decay, s_grad), "seq", link_states, identity, True)[1]
    dx_four = jnp.einsum("ghts,tghp->sghp", mixed, dy_four, preferred_element_type=jnp.float32)
    dx_four = dx_four + ends.transpose(2, 0, 1)[..., None] * jnp.einsum(
        "sgn,ghpn->sghp", b_f32, rsum, precision=HIGH
    )
    grad_x = dx_four.astype(jnp.bfloat16).reshape(rows, heads * width)
    dgram = jnp.sum(
        jnp.einsum("tghp,sghp->ghts", dy_four, x_four, preferred_element_type=jnp.float32) * w_four,
        axis=1,
    )
    dgram_half = dgram.astype(jnp.bfloat16)
    db = jnp.einsum("gts,tgn->sgn", dgram_half, c_mat, preferred_element_type=jnp.float32)
    db = db + jnp.einsum("ghs,sghp,ghpn->sgn", ends, x_f32, rsum, precision=HIGH)
    dc = jnp.einsum("gts,sgn->tgn", dgram_half, b_mat, preferred_element_type=jnp.float32)
    dc = dc + jnp.einsum("ght,tghp,ghpn->tgn", entry, dy_f32, s_in, precision=HIGH)
    dproj = jnp.stack([db, dc], axis=2).astype(jnp.bfloat16).reshape(rows, groups * 2 * nstate)
    incomplete_figure = jnp.einsum(
        "td,tc->dc", hidden_in, dproj, preferred_element_type=jnp.float32
    )
    fixed, exponent = quantized(incomplete_figure)
    mantissa = lax.psum_scatter(
        fixed.astype(jnp.bfloat16), "seq", scatter_dimension=0, tiled=True
    ).astype(jnp.float32)
    return (y_out, grad_x, mantissa * 2.0 ** (-20), exponent)


def solution(mesh):
    in_specs = (P(), P("seq", None), P("seq", "mp"), P("seq", "mp"), P("seq", "mp"), P("seq", "mp"))
    out_specs = (P("seq", "mp"), P("seq", "mp"), P("seq", "mp"), P())
    return jax.shard_map(shards, mesh=mesh, in_specs=in_specs, out_specs=out_specs, check_vma=False)
```

profile of v0, /device:TPU:0, one launch (start us, length us, event | category | flops | bytes accessed | tf_op | source)
XLA Modules:
  0.0 536.4 jit_solution(18159369142180270509)
XLA Ops:
  7.2 0.7 all-gather.7.cloned.1.call-update
  8.0 1.2 reduce-window.33
  9.4 0.8 reduce-window.30
  10.2 0.7 bitcast_subtract_fusion
  11.0 0.3 reduce-window.31
  11.4 2.9 copy.61
  15.1 68.2 %all-gather.7.cloned.1.call-done = bf16[8192,512]{1,0:T(8,128)(2,1)} async-done(((bf16[512,512]{1,0:T(8,128)(2,1)}), bf16[8192,512]{1,0:T(8,128)(2,1)}) %all-gather.7.cloned.1.call-update) | async-done | bytes 8388624 | tf_op jit(solution)/shard_map/all_gather | solution.py:71
  83.3 10.3 %convolution_convert_fusion = bf16[512,512]{0,1:T(8,128)(2,1)S(1)} fusion(bf16[512,8192]{1,0:T(8,128)(2,1)} %param.11, bf16[8192,512]{1,0:T(8,128)(2,1)} %all-gather.7.cloned.1.call-done), kind=kOutput, calls=%fused_computation.46 | convolution fusion | flops 4295229440 | bytes 17301504 | tf_op jit(solution)/shard_map/dot_general | solution.py:69
  93.6 3.3 fusion.31
  96.9 3.9 copy.67
  100.9 4.9 fusion.32
  106.1 30.5 %all-gather = bf16[16,32,1]{1,2,0:T(2,128)(2,1)S(1)} all-gather(bf16[1,32,1]{1,2,0:T(2,128)(2,1)S(1)} %copy.63), channel_id=2, replica_groups=mesh['seq'=16,'mp'=8] {'seq'}, dimensions={0}, use_global_device_ids=true | all-gather | bytes 1088 | tf_op jit(solution)/shard_map/all_gather | solution.py:18
  136.7 11.8 %multiply_reduce_fusion = bf16[512,512]{1,0:T(8,128)(2,1)S(1)} fusion(f32[32,512]{1,0:T(8,128)S(1)} %bitcast.218, pred[512,512]{1,0:T(8,128)(4,1)S(1)} %fusion.57, bf16[512,32,64]{0,2,1:T(8,128)(2,1)} %bitcast.201, bf16[512,32,64]{0,2,1:T(8,128)(2,1)S(1)} %bitcast.197), kind=kOutput, calls=%fused_computation.4 | convolution fusion | flops 1107034112 | bytes 5046272 | tf_op jit(solution)/shard_map/tghp,sghp->ghts/dot_general | solution.py:101
  148.5 1.1 convolution_bitcast_fusion
  149.6 0.3 convolution_bitcast_fusion.1
  149.9 58.0 %all-gather.9.cloned.1.call-done = bf16[512,64,256]{2,1,0:T(8,128)(2,1)} async-done(((bf16[32,64,256]{2,1,0:T(8,128)(2,1)}), bf16[512,64,256]{2,1,0:T(8,128)(2,1)}) %all-gather.9.cloned.1.call-update) | async-done | bytes 16777232 | tf_op jit(solution)/shard_map/all_gather | solution.py:18
  208.2 112.8 %all-gather.11.cloned.1.call-done = bf16[512,64,256]{2,1,0:T(8,128)(2,1)} async-done(((bf16[32,64,256]{2,1,0:T(8,128)(2,1)}), bf16[512,64,256]{2,1,0:T(8,128)(2,1)}) %all-gather.11.cloned.1.call-update) | async-done | bytes 16777232 | tf_op jit(solution)/shard_map/all_gather | solution.py:18
  321.3 25.2 %while.27 = (s32[]{:T(128)}, f32[1,32,64,256]{3,2,1,0:T(8,128)S(1)}, s32[]{:T(128)}, bf16[16,1,32]{2,1,0:T(2,128)(2,1)S(1)}, bf16[16,1,32,64,256]{4,3,2,1,0:T(8,...) while((s32[]{:T(128)}, f32[1,32,64,256]{3,2,1,0:T(8,128)S(1)}, s32[]{:T(128)}, ...), condition=%wide.region_9.10_spmd, body=%wide.region_8.9_spmd.sunk | while | flops 1572902 | bytes 5243355 | solution.py:33
  321.3 1.6 convert_add_fusion.5
  323.0 1.6 convert_add_fusion.5
  324.7 1.6 convert_add_fusion.5
  326.3 1.6 convert_add_fusion.5
  328.0 1.6 convert_add_fusion.5
  329.7 1.6 convert_add_fusion.5
  331.4 1.6 convert_add_fusion.5
  333.1 1.6 convert_add_fusion.5
  334.7 1.6 convert_add_fusion.5
  336.4 1.6 convert_add_fusion.5
  338.1 1.6 convert_add_fusion.5
  339.8 1.6 convert_add_fusion.5
  341.4 1.6 convert_add_fusion.5
  343.1 1.6 convert_add_fusion.5
  344.8 1.6 convert_add_fusion.5
  346.5 6.5 %fusion.51 = bf16[512,1,1,256]{0,3,2,1:T(8,128)(2,1)S(1)} fusion(f32[512,1,256]{0,2,1:T(8,128)} %convolution_bitcast_fusion, f32[1,32,64,256]{3,2,1,0:T(8,128)} %copy-done.2, bf16[512,32,64]{0,2,1:T(8,128)(2,1)} %bitcast.202, f32[512,32]{0,1:T(8,128)} %copy-done.12), kind=kOutput, calls=%fused_computation.55 | convolution fusion | flops 3223584768 | bytes 5046272 | tf_op jit(solution)/shard_map/ght,tghp,ghpn->tgn/dot_general | solution.py:108
  353.0 4.1 fusion.54
  357.2 12.2 %abs_reduce_fusion = (f32[]{:T(128)}, f32[512,8192]{1,0:T(8,128)}) fusion(bf16[512,512]{0,1:T(8,128)(2,1)S(1)} %bitcast.211, bf16[512,8192]{1,0:T(8,128)(2,1)} %param.11), kind=kOutput, calls=%fused_computation.10 | convolution fusion | flops 4303355904 | bytes 25690116 | tf_op jit(solution)/shard_map/td,tc->dc/dot_general | solution.py:110
  369.4 64.8 %pmax.7 = f32[]{:T(128)} all-reduce(f32[]{:T(128)} %get-tuple-element.214), channel_id=1, replica_groups=mesh['seq'=16,'mp'=8] {'seq','mp'}, use_global_device_ids=true, to_apply=%region_12.13 | all-reduce | flops 1 | bytes 8 | tf_op jit(solution)/shard_map/pmax | solution.py:41
  434.9 9.5 %fusion.12 = bf16[8192,512]{0,1:T(8,128)(2,1)} fusion(f32[512,8192]{1,0:T(8,128)} %get-tuple-element.215, f32[]{:T(128)S(6)} %exp2.7), kind=kLoop, calls=%fused_computation.21 | loop fusion | flops 16777216 | bytes 25165828 | tf_op jit(solution)/shard_map/convert_element_type | solution.py:115
  444.5 0.3 fusion.63
  444.9 4.0 fusion.25
  448.9 11.0 %fusion.16 = bf16[512,1,32,64]{0,3,2,1:T(8,128)(2,1)} fusion(f32[32,64,512]{2,1,0:T(8,128)S(1)} %fusion.25, bf16[512,32,64]{0,2,1:T(8,128)(2,1)S(1)} %bitcast.199, f32[32,512]{1,0:T(8,128)S(1)} %bitcast.219, f32[512,512]{1,0:T(8,128)S(1)} %fusion.63, pred[512,512]{1,0:T(8,128)(4,1)S(1)} %fusion.57, f32[512,32]{0,1:T(8,128)S(1)} %fusion.89), kind=kOutput, calls=%fused_computation.27 | convolution fusion | flops 1110441984 | bytes 9830400 | tf_op jit(solution)/shard_map/ghts,sghp->tghp/dot_general | solution.py:88
  459.9 3.9 copy.70
  463.9 1.8 fusion.22
  465.9 8.7 %fusion.14 = bf16[512,1,32,64]{0,3,2,1:T(8,128)(2,1)S(1)} fusion(f32[32,64,512]{2,1,0:T(8,128)S(1)} %fusion.22, bf16[512,32,64]{0,2,1:T(8,128)(2,1)S(1)} %bitcast.203, f32[32,512]{1,0:T(8,128)S(1)} %bitcast.220, f32[512,512]{1,0:T(8,128)S(1)} %copy-done.8, pred[512,512]{1,0:T(8,128)(4,1)S(1)} %fusion.57, f32[512,32]{0,1:T(8,128)S(1)} %copy-done.11), kind=kOutput, calls=%fused_computation.24 | convolution fusion | flops 1110441984 | bytes 9830400 | tf_op jit(solution)/shard_map/ghts,tghp->sghp/dot_general | solution.py:95
  474.6 2.4 copy.71
  477.0 48.9 %reduce-scatter.2.cloned.1.call-done = bf16[512,512]{0,1:T(8,128)(2,1)} async-done(((bf16[8192,512]{0,1:T(8,128)(2,1)}), bf16[512,512]{0,1:T(8,128)(2,1)}) %reduce-scatter.2.cloned.1.call-update) | async-done | bytes 524304 | tf_op jit(solution)/shard_map/reduce_scatter | solution.py:114
  525.8 1.2 convert_multiply_fusion.26
  527.0 1.3 copy.72
  (77 shorter events, 2.6 us)
Async XLA Ops:
  7.2 0.8 copy-start
  7.2 76.1 %all-gather.7.cloned.1.call-start = ((), (), s32[]{:S(2)}) async-start(), calls=%async_computation.1 | async-start | bytes 8912896 | tf_op jit(solution)/shard_map/all_gather | solution.py:71
  7.9 200.0 %all-gather.9.cloned.1.call-start = ((), (), s32[]{:S(2)}) async-start(), calls=%async_computation.3 | async-start | bytes 17825792 | tf_op jit(solution)/shard_map/all_gather | solution.py:18
  14.3 122.4 %copy-start.3 = (bf16[512,2048]{0,1:T(8,128)(2,1)}, bf16[512,2048]{0,1:T(8,128)(2,1)S(1)}, u32[]{:S(2)}) copy-start(bf16[512,2048]{0,1:T(8,128)(2,1)S(1)} %copy.61) | copy-start | bytes 6291460
  15.1 78.5 %copy-start.9 = (f32[512,32]{0,1:T(8,128)}, f32[512,32]{0,1:T(8,128)S(1)}, u32[]{:S(2)}) copy-start(f32[512,32]{0,1:T(8,128)S(1)} %exponential_bitcast_fusion) | copy-start | bytes 196612
  96.9 224.2 %all-gather.11.cloned.1.call-start = ((), (), s32[]{:S(2)}) async-start(), calls=%async_computation.4 | async-start | bytes 17825792 | tf_op jit(solution)/shard_map/all_gather | solution.py:18
  100.9 47.6 %copy-start.12 = (f32[512,32]{0,1:T(8,128)}, f32[512,32]{0,1:T(8,128)S(1)}, u32[]{:S(2)}) copy-start(f32[512,32]{0,1:T(8,128)S(1)} %multiply_bitcast_fusion) | copy-start | bytes 196612
  105.8 420.1 %reduce-scatter.2.cloned.1.call-start = ((), (), s32[]{:S(2)}) async-start(), calls=%async_computation.2 | async-start | bytes 8912896 | tf_op jit(solution)/shard_map/reduce_scatter | solution.py:114
  208.2 112.8 %copy-start.2 = (f32[1,32,64,256]{3,2,1,0:T(8,128)}, f32[1,32,64,256]{3,2,1,0:T(8,128)S(1)}, u32[]{:S(2)}) copy-start(f32[1,32,64,256]{3,2,1,0:T(8,128)S(1)} %get-tuple-element.132) | copy-start | bytes 6291460
  346.5 6.6 %copy-start.4 = (bf16[512,2048]{0,1:T(8,128)(2,1)S(1)}, bf16[512,2048]{0,1:T(8,128)(2,1)}, u32[]{:S(2)}) copy-start(bf16[512,2048]{0,1:T(8,128)(2,1)} %copy-done.3) | copy-start | bytes 6291460
  346.5 6.6 %copy-start.10 = (f32[512,32]{0,1:T(8,128)S(1)}, f32[512,32]{0,1:T(8,128)}, u32[]{:S(2)}) copy-start(f32[512,32]{0,1:T(8,128)} %copy-done.9) | copy-start | bytes 196612
  444.5 4.4 copy-start.5
  444.8 15.1 %copy-start.7 = (f32[512,512]{1,0:T(8,128)}, f32[512,512]{1,0:T(8,128)S(1)}, u32[]{:S(2)}) copy-start(f32[512,512]{1,0:T(8,128)S(1)} %fusion.63) | copy-start | bytes 3145732
  463.9 1.8 copy-start.6
  463.9 2.0 copy-start.8
  463.9 2.0 copy-start.11
  465.9 62.5 %copy-start.1 = (f32[512,32]{0,1:T(8,128)S(1)}, f32[512,32]{0,1:T(8,128)}, u32[]{:S(2)}) copy-start(f32[512,32]{0,1:T(8,128)} %param.14) | copy-start | bytes 196612
Sparse Core Ops, SparseCore 0:
  10.2 73.0 all-gather.6
  97.0 110.8 all-gather.8
  210.1 110.8 all-gather.10
  444.6 81.1 reduce-scatter.1
where the time goes:
time: 545 us; the launch traced here: 536 us
  waiting for transfers between devices  289 us (53%)
  blocking collectives  95.3 us (17%)
  matrix products  80.4 us (15%)
  other arithmetic  39.1 us (7%)
  between operations  16.3 us (3%)
  local copies, waits for them, and re-layouts  15.9 us (3%)
    all_gather x2, waiting for transfers between devices, prefix(): lax.all_gather(a.astype(kind), axis)  171 us
    all_gather x1, waiting for transfers between devices, shards(): lax.all_gather(w_bc, 'seq', axis=0, tiled=True)  68.2 us
    pmax x1, blocking collectives, quantized(): largest = lax.pmax(jnp.max(jnp.abs(incomplete_figure)), ('seq', 'mp'))  64.8 us
    reduce_scatter x1, waiting for transfers between devices, shards(): lax.psum_scatter(fixed.astype(jnp.bfloat16), 'seq', scatter_dimension=0,...  48.9 us
    all_gather x1, blocking collectives, prefix(): lax.all_gather(a.astype(kind), axis)  30.5 us
    add x15, other arithmetic, link_states(): later[0][:, :, None, None] * earlier[1] + later[1]  24.6 us
    unnamed x32, local copies, waits for them, and re-layouts  14.8 us
    dot_general x1, matrix products, shards(): jnp.einsum('td,tc->dc', hidden_in, dproj, preferred_element_type=jnp.floa...  12.2 us
  transfers between devices with their start and end apart: 4, of which 4 were waited for; matrix products, arithmetic and copies ran while one was open for 12% of the time, Pallas kernels for 0%

commit v1 on v0

--- a/solution.py
+++ b/solution.py
@@ -1,7 +1,193 @@
+import functools
 import jax
 import jax.numpy as jnp
 from jax import lax
+from jax.experimental import pallas as pl
+from jax.experimental.pallas import tpu as pltpu
 from jax.sharding import PartitionSpec as P
+
+MESH = pl.DeviceIdType.MESH
+MB = 1 << 20
+
+
+def place():
+    i = lax.axis_index("seq")
+    return i, i // 4, lax.rem(i, 4), lax.axis_index("mp")
+
+
+def at(x, y, dx, dy):
+    return lax.rem(x + dx + 4, 4) * 4 + lax.rem(y + dy + 4, 4)
+
+
+def step_of(half, da, db):
+    return (db, da) if half == 0 else (da, db)
+
+
+def gather_plan():
+    plan = {}
+    for da in (0, 1, -1, 2):
+        if da:
+            for q in (0, 1) if abs(da) == 2 else (None,):
+                plan[("a", da, 0, q)] = len(plan)
+        for db in (1, -1):
+            plan[("b", da, db, None)] = len(plan)
+        for q in (0, 1):
+            plan[("b", da, 2, q)] = len(plan)
+    return plan
+
+
+PLAN = gather_plan()
+
+
+def gather_kernel(hid, w, proj, hbuf, wbuf, acc, hsem, ssem, rsem):
+    i, x, y, j = place()
+    load = pltpu.make_async_copy(hid, hbuf, hsem.at[0])
+    load.start()
+
+    def owner(half, da, db):
+        dx, dy = step_of(half, da, db)
+        return at(x, y, dx, dy)
+
+    def device(half, axis, sign):
+        da, db = (sign, 0) if axis == "a" else (0, sign)
+        return (owner(half, da, db), j)
+
+    barrier = pltpu.get_barrier_semaphore()
+    for axis in "ab":
+        for sign in (1, -1):
+            pl.semaphore_signal(barrier, inc=1, device_id=device(0, axis, sign), device_id_type=MESH)
+    pl.semaphore_wait(barrier, 4)
+
+    def rows(half, q):
+        return pl.ds(256 * half, 256) if q is None else pl.ds(256 * half + 128 * q, 128)
+
+    def copy(half, axis, da, db, q, sign):
+        m = PLAN[(axis, da, db, q)]
+        if axis == "a":
+            oa = da - (-sign) if abs(da) == 1 else -sign
+            ob = 0
+        else:
+            oa = da
+            ob = 0 if abs(db) == 1 else -sign
+        k = owner(half, oa, ob)
+        src = w if (oa, ob) == (0, 0) else wbuf.at[k]
+        return pltpu.make_async_remote_copy(
+            src_ref=src.at[rows(half, q), :],
+            dst_ref=wbuf.at[k, rows(half, q), :],
+            send_sem=ssem.at[half, m],
+            recv_sem=rsem.at[half, m],
+            device_id=device(half, axis, sign),
+            device_id_type=MESH,
+        )
+
+    sent = []
+
+    def send(half, axis, da, db, q, sign):
+        c = copy(half, axis, da, db, q, sign)
+        c.start()
+        sent.append(c)
+
+    def got(half, axis, da, db, q):
+        sign = -1 if (da if axis == "a" else db) > 0 else 1
+        if abs(da if axis == "a" else db) == 2:
+            sign = 1 if q == 0 else -1
+        k = owner(half, da, db)
+        m = PLAN[(axis, da, db, q)]
+        ref = wbuf.at[k, rows(half, q), :]
+        pltpu.make_async_remote_copy(
+            src_ref=ref, dst_ref=ref, send_sem=ssem.at[half, m], recv_sem=rsem.at[half, m],
+            device_id=device(half, axis, sign), device_id_type=MESH,
+        ).wait_recv()
+
+    def out_b(half, da):
+        send(half, "b", da, -1, None, 1)
+        send(half, "b", da, 1, None, -1)
+
+    def fwd_b(half, da):
+        got(half, "b", da, -1, None)
+        send(half, "b", da, 2, 0, 1)
+        got(half, "b", da, 1, None)
+        send(half, "b", da, 2, 1, -1)
+
+    def mul(pairs, src=None):
+        def one(n, _):
+            half, r = lax.rem(n, 2), n // 2
+            da = sum(jnp.where(r == t, p[0], 0) for t, p in enumerate(pairs))
+            db = sum(jnp.where(r == t, p[1], 0) for t, p in enumerate(pairs))
+            dx = jnp.where(half == 0, db, da)
+            dy = jnp.where(half == 0, da, db)
+            k = at(x, y, dx, dy)
+            off = pl.multiple_of(half * 256, 256)
+            cols = pl.ds(pl.multiple_of(k * 512 + off, 256), 256)
+            if src is None:
+                b = wbuf[k, pl.ds(off, 256), :]
+            else:
+                b = src[pl.ds(off, 256), :]
+            acc[...] += jnp.dot(hbuf[:, cols], b, preferred_element_type=jnp.float32)
+            return 0
+
+        lax.fori_loop(0, 2 * len(pairs), one, 0)
+
+    for half in (0, 1):
+        send(half, "a", -1, 0, None, 1)
+        send(half, "a", 1, 0, None, -1)
+    for half in (0, 1):
+        out_b(half, 0)
+    acc[...] = jnp.zeros_like(acc)
+    load.wait()
+    mul([(0, 0)], w)
+    for half in (0, 1):
+        got(half, "a", -1, 0, None)
+        send(half, "a", 2, 0, 0, 1)
+        got(half, "a", 1, 0, None)
+        send(half, "a", 2, 0, 1, -1)
+    for half in (0, 1):
+        out_b(half, -1)
+        out_b(half, 1)
+    for half in (0, 1):
+        fwd_b(half, 0)
+    mul([(-1, 0), (1, 0)])
+    for half in (0, 1):
+        got(half, "a", 2, 0, 0)
+        got(half, "a", 2, 0, 1)
+        out_b(half, 2)
+    mul([(0, -1), (0, 1), (2, 0)])
+    for half in (0, 1):
+        fwd_b(half, -1)
+        fwd_b(half, 1)
+    mul([(-1, -1), (-1, 1), (1, -1), (1, 1)])
+    for half in (0, 1):
+        fwd_b(half, 2)
+    mul([(2, -1), (2, 1)])
+    for da in (0, -1, 1, 2):
+        for half in (0, 1):
+            got(half, "b", da, 2, 0)
+            got(half, "b", da, 2, 1)
+        mul([(da, 2)])
+    for c in sent:
+        c.wait_send()
+    proj[...] = acc[...].astype(jnp.bfloat16)
+
+
+def gather_proj(hidden, w):
+    n = len(PLAN)
+    return pl.pallas_call(
+        gather_kernel,
+        out_shape=jax.ShapeDtypeStruct((512, 512), jnp.bfloat16),
+        in_specs=[pl.BlockSpec(memory_space=pl.ANY), pl.BlockSpec(memory_space=pltpu.VMEM)],
+        out_specs=pl.BlockSpec(memory_space=pltpu.VMEM),
+        scratch_shapes=[
+            pltpu.VMEM((512, 8192), jnp.bfloat16),
+            pltpu.VMEM((16, 512, 512), jnp.bfloat16),
+            pltpu.VMEM((512, 512), jnp.float32),
+            pltpu.SemaphoreType.DMA((1,)),
+            pltpu.SemaphoreType.DMA((2, n)),
+            pltpu.SemaphoreType.DMA((2, n)),
+        ],
+        compiler_params=pltpu.CompilerParams(collective_id=0, has_side_effects=True, vmem_limit_bytes=56 * MB),
+        name="gather_proj",
+    )(hidden, w)
+
 
 HEADS = 256
 GROUPS = 8
@@ -66,12 +252,8 @@
     )
     ends = w_four[:, :, -1, :]
     decay = entry[:, :, -1]
-    proj = jnp.dot(
-        hidden_in,
-        lax.all_gather(w_bc, "seq", axis=0, tiled=True),
-        preferred_element_type=jnp.float32,
-    )
-    pairs = proj.astype(jnp.bfloat16).reshape(rows, groups, 2, nstate)
+    proj = gather_proj(hidden_in, w_bc)
+    pairs = proj.reshape(rows, groups, 2, nstate)
     b_mat = pairs[:, :, 0, :]
     c_mat = pairs[:, :, 1, :]
     b_f32 = b_mat.astype(jnp.float32)

time: 545 us -> 521 us (0.956)
  waiting for transfers between devices: 289 us -> 221 us
  Pallas kernels: 0 us -> 52 us
  matrix products: 80.4 us -> 70 us
    all_gather x1 -> x0, waiting for transfers between devices: 68.2 us -> none  [shards(): lax.all_gather(w_bc, 'seq', axis=0, tiled=True)]
    pallas_call x0 -> x1, Pallas kernels: none -> 52 us  [gather_proj(): pl.pallas_call(gather_kernel, out_shape=jax.ShapeDtypeStruct((512, 512),...]
    dot_general x1 -> x0, matrix products: 10.3 us -> none  [shards(): jnp.dot(hidden_in, lax.all_gather(w_bc, 'seq', axis=0, tiled=True), prefe...]
    unnamed x32 -> x36, local copies, waits for them, and re-layouts: 14.8 us -> 15.6 us
  transfers between devices with their start and end apart: 4 -> 3, of which waited for: 4 -> 3; matrix products, arithmetic and copies ran while one was open for 12% -> 11% of each run, Pallas kernels for 0% -> 0%
where the time goes in v1:
time: 521 us; the launch traced here: 513 us
  waiting for transfers between devices  221 us (42%)
  blocking collectives  93.8 us (18%)
  matrix products  70 us (13%)
  Pallas kernels  52 us (10%)
  other arithmetic  39.7 us (8%)
  local copies, waits for them, and re-layouts  18.7 us (4%)
  between operations  16.4 us (3%)
    all_gather x2, waiting for transfers between devices, prefix(): lax.all_gather(a.astype(kind), axis)  172 us
    pmax x1, blocking collectives, quantized(): largest = lax.pmax(jnp.max(jnp.abs(incomplete_figure)), ('seq', 'mp'))  64.8 us
    pallas_call x1, Pallas kernels, gather_proj(): pl.pallas_call(gather_kernel, out_shape=jax.ShapeDtypeStruct((512, 512),...  52 us
    reduce_scatter x1, waiting for transfers between devices, shards(): lax.psum_scatter(fixed.astype(jnp.bfloat16), 'seq', scatter_dimension=0,...  49 us
    all_gather x1, blocking collectives, prefix(): lax.all_gather(a.astype(kind), axis)  29 us
    add x15, other arithmetic, link_states(): later[0][:, :, None, None] * earlier[1] + later[1]  24.6 us
    unnamed x36, local copies, waits for them, and re-layouts  15.6 us
    dot_general x1, matrix products, shards(): jnp.einsum('td,tc->dc', hidden_in, dproj, preferred_element_type=jnp.floa...  12.2 us
  transfers between devices with their start and end apart: 3, of which 3 were waited for; matrix products, arithmetic and copies ran while one was open for 11% of the time, Pallas kernels for 0%

profile of v1, /device:TPU:0, one launch (start us, length us, event | category | flops | bytes accessed | tf_op | source)
XLA Modules:
  0.0 512.6 jit_solution(5531064379216062652)
XLA Ops:
  7.2 0.8 copy-done
  8.0 1.2 reduce-window.33
  9.4 0.7 add_bitcast_fusion
  10.1 0.8 reduce-window.30
  11.0 0.7 bitcast_subtract_fusion
  12.3 2.9 copy.61
  15.6 52.0 %gather_proj.1 = bf16[512,512]{1,0:T(8,128)(2,1)} custom-call(bf16[512,8192]{1,0:T(8,128)(2,1)} %hid.1, bf16[512,512]{1,0:T(8,128)(2,1)} %w.1), custom_call_target="tpu_custom_call" | custom-call | tf_op jit(solution)/shard_map/gather_proj/pallas_call | solution.py:174
  67.6 1.2 reshape.424
  68.8 0.7 fusion.71
  69.7 3.2 fusion.31
  73.1 4.0 copy.67
  77.0 4.9 fusion.32
  82.3 29.0 %all-gather = bf16[16,32,1]{1,2,0:T(2,128)(2,1)S(1)} all-gather(bf16[1,32,1]{1,2,0:T(2,128)(2,1)S(1)} %copy.63), channel_id=2, replica_groups=mesh['seq'=16,'mp'=8] {'seq'}, dimensions={0}, use_global_device_ids=true | all-gather | bytes 1088 | tf_op jit(solution)/shard_map/all_gather | solution.py:204
  111.3 11.6 %multiply_reduce_fusion = bf16[512,512]{1,0:T(8,128)(2,1)S(1)} fusion(f32[32,512]{1,0:T(8,128)S(1)} %bitcast.200, pred[512,512]{1,0:T(8,128)(4,1)S(1)} %fusion.57, bf16[512,32,64]{0,2,1:T(8,128)(2,1)} %bitcast.190, bf16[512,32,64]{0,2,1:T(8,128)(2,1)S(1)} %bitcast.186), kind=kOutput, calls=%fused_computation.4 | convolution fusion | flops 1107034112 | bytes 5046272 | tf_op jit(solution)/shard_map/tghp,sghp->ghts/dot_general | solution.py:283
  123.0 1.1 convolution_bitcast_fusion
  124.4 59.5 %all-gather.6.cloned.1.call-done = bf16[512,64,256]{2,1,0:T(8,128)(2,1)} async-done(((bf16[32,64,256]{2,1,0:T(8,128)(2,1)}), bf16[512,64,256]{2,1,0:T(8,128)(2,1)}) %all-gather.6.cloned.1.call-update) | async-done | bytes 16777232 | tf_op jit(solution)/shard_map/all_gather | solution.py:204
  184.2 112.8 %all-gather.8.cloned.1.call-done = bf16[512,64,256]{2,1,0:T(8,128)(2,1)} async-done(((bf16[32,64,256]{2,1,0:T(8,128)(2,1)}), bf16[512,64,256]{2,1,0:T(8,128)(2,1)}) %all-gather.8.cloned.1.call-update) | async-done | bytes 16777232 | tf_op jit(solution)/shard_map/all_gather | solution.py:204
  297.3 25.2 %while.27 = (s32[]{:T(128)}, f32[1,32,64,256]{3,2,1,0:T(8,128)S(1)}, s32[]{:T(128)}, bf16[16,1,32]{2,1,0:T(2,128)(2,1)S(1)}, bf16[16,1,32,64,256]{4,3,2,1,0:T(8,...) while((s32[]{:T(128)}, f32[1,32,64,256]{3,2,1,0:T(8,128)S(1)}, s32[]{:T(128)}, ...), condition=%wide.region_9.10_spmd, body=%wide.region_8.9_spmd.sunk | while | flops 1572902 | bytes 5243355 | solution.py:219
  297.3 1.6 convert_add_fusion.5
  299.0 1.6 convert_add_fusion.5
  300.7 1.6 convert_add_fusion.5
  302.4 1.6 convert_add_fusion.5
  304.0 1.6 convert_add_fusion.5
  305.7 1.6 convert_add_fusion.5
  307.4 1.6 convert_add_fusion.5
  309.1 1.6 convert_add_fusion.5
  310.7 1.6 convert_add_fusion.5
  312.4 1.6 convert_add_fusion.5
  314.1 1.6 convert_add_fusion.5
  315.8 1.6 convert_add_fusion.5
  317.5 1.6 convert_add_fusion.5
  319.1 1.6 convert_add_fusion.5
  320.8 1.6 convert_add_fusion.5
  322.5 6.5 %fusion.51 = bf16[512,1,1,256]{0,3,2,1:T(8,128)(2,1)S(1)} fusion(f32[512,1,256]{0,2,1:T(8,128)} %convolution_bitcast_fusion, f32[1,32,64,256]{3,2,1,0:T(8,128)} %copy-done.2, bf16[512,32,64]{0,2,1:T(8,128)(2,1)} %bitcast.191, f32[512,32]{0,1:T(8,128)} %copy-done.12), kind=kOutput, calls=%fused_computation.54 | convolution fusion | flops 3223584768 | bytes 5046272 | tf_op jit(solution)/shard_map/ght,tghp,ghpn->tgn/dot_general | solution.py:290
  329.1 4.1 fusion.54
  333.2 12.2 %abs_reduce_fusion = (f32[]{:T(128)}, f32[512,8192]{1,0:T(8,128)}) fusion(bf16[512,512]{0,1:T(8,128)(2,1)S(1)} %bitcast.193, bf16[512,8192]{1,0:T(8,128)(2,1)} %hid.1), kind=kOutput, calls=%fused_computation.10 | convolution fusion | flops 4303355904 | bytes 25690116 | tf_op jit(solution)/shard_map/td,tc->dc/dot_general | solution.py:292
  345.4 64.8 %pmax.7 = f32[]{:T(128)} all-reduce(f32[]{:T(128)} %get-tuple-element.216), channel_id=1, replica_groups=mesh['seq'=16,'mp'=8] {'seq','mp'}, use_global_device_ids=true, to_apply=%region_12.13 | all-reduce | flops 1 | bytes 8 | tf_op jit(solution)/shard_map/pmax | solution.py:227
  410.9 9.5 %fusion.12 = bf16[8192,512]{0,1:T(8,128)(2,1)} fusion(f32[512,8192]{1,0:T(8,128)} %get-tuple-element.217, f32[]{:T(128)S(6)} %exp2.7), kind=kLoop, calls=%fused_computation.21 | loop fusion | flops 16777216 | bytes 25165828 | tf_op jit(solution)/shard_map/convert_element_type | solution.py:297
  420.5 0.3 fusion.63
  420.9 4.1 fusion.25
  425.0 11.0 %fusion.16 = bf16[512,1,32,64]{0,3,2,1:T(8,128)(2,1)} fusion(f32[32,64,512]{2,1,0:T(8,128)S(1)} %fusion.25, bf16[512,32,64]{0,2,1:T(8,128)(2,1)S(1)} %bitcast.188, f32[32,512]{1,0:T(8,128)S(1)} %bitcast.201, f32[512,512]{1,0:T(8,128)S(1)} %fusion.63, pred[512,512]{1,0:T(8,128)(4,1)S(1)} %fusion.57, f32[512,32]{0,1:T(8,128)S(1)} %fusion.80), kind=kOutput, calls=%fused_computation.27 | convolution fusion | flops 1110441984 | bytes 9830400 | tf_op jit(solution)/shard_map/ghts,sghp->tghp/dot_general | solution.py:270
  436.0 3.9 copy.70
  440.0 1.8 fusion.22
  442.0 8.7 %fusion.14 = bf16[512,1,32,64]{0,3,2,1:T(8,128)(2,1)S(1)} fusion(f32[32,64,512]{2,1,0:T(8,128)S(1)} %fusion.22, bf16[512,32,64]{0,2,1:T(8,128)(2,1)S(1)} %bitcast.192, f32[32,512]{1,0:T(8,128)S(1)} %bitcast.202, f32[512,512]{1,0:T(8,128)S(1)} %copy-done.8, pred[512,512]{1,0:T(8,128)(4,1)S(1)} %fusion.57, f32[512,32]{0,1:T(8,128)S(1)} %copy-done.11), kind=kOutput, calls=%fused_computation.24 | convolution fusion | flops 1110441984 | bytes 9830400 | tf_op jit(solution)/shard_map/ghts,tghp->sghp/dot_general | solution.py:277
  450.6 2.4 copy.71
  453.0 49.0 %reduce-scatter.2.cloned.1.call-done = bf16[512,512]{0,1:T(8,128)(2,1)} async-done(((bf16[8192,512]{0,1:T(8,128)(2,1)}), bf16[512,512]{0,1:T(8,128)(2,1)}) %reduce-scatter.2.cloned.1.call-update) | async-done | bytes 524304 | tf_op jit(solution)/shard_map/reduce_scatter | solution.py:296
  502.1 1.2 convert_multiply_fusion.26
  503.2 1.3 copy.72
  (80 shorter events, 3.1 us)
Async XLA Ops:
  7.2 0.8 copy-start
  7.2 176.8 %all-gather.6.cloned.1.call-start = ((), (), s32[]{:S(2)}) async-start(), calls=%async_computation.2 | async-start | bytes 17825792 | tf_op jit(solution)/shard_map/all_gather | solution.py:204
  15.2 96.1 %copy-start.3 = (bf16[512,2048]{0,1:T(8,128)(2,1)}, bf16[512,2048]{0,1:T(8,128)(2,1)S(1)}, u32[]{:S(2)}) copy-start(bf16[512,2048]{0,1:T(8,128)(2,1)S(1)} %copy.61) | copy-start | bytes 6291460
  69.7 3.3 copy-start.9
  72.9 224.1 %all-gather.8.cloned.1.call-start = ((), (), s32[]{:S(2)}) async-start(), calls=%async_computation.3 | async-start | bytes 17825792 | tf_op jit(solution)/shard_map/all_gather | solution.py:204
  73.0 8.9 %copy-start.13 = (f32[32,4,128]{2,0,1:T(8,128)S(1)}, f32[32,4,128]{2,0,1:T(8,128)}, u32[]{:S(2)}) copy-start(f32[32,4,128]{2,0,1:T(8,128)} %get-tuple-element.215) | copy-start | bytes 196612
  77.0 45.9 %copy-start.12 = (f32[512,32]{0,1:T(8,128)}, f32[512,32]{0,1:T(8,128)S(1)}, u32[]{:S(2)}) copy-start(f32[512,32]{0,1:T(8,128)S(1)} %multiply_bitcast_fusion) | copy-start | bytes 196612
  81.9 420.1 %reduce-scatter.2.cloned.1.call-start = ((), (), s32[]{:S(2)}) async-start(), calls=%async_computation.1 | async-start | bytes 8912896 | tf_op jit(solution)/shard_map/reduce_scatter | solution.py:296
  184.2 112.8 %copy-start.2 = (f32[1,32,64,256]{3,2,1,0:T(8,128)}, f32[1,32,64,256]{3,2,1,0:T(8,128)S(1)}, u32[]{:S(2)}) copy-start(f32[1,32,64,256]{3,2,1,0:T(8,128)S(1)} %get-tuple-element.132) | copy-start | bytes 6291460
  322.5 6.6 %copy-start.4 = (bf16[512,2048]{0,1:T(8,128)(2,1)S(1)}, bf16[512,2048]{0,1:T(8,128)(2,1)}, u32[]{:S(2)}) copy-start(bf16[512,2048]{0,1:T(8,128)(2,1)} %copy-done.3) | copy-start | bytes 6291460
  322.5 6.6 %copy-start.10 = (f32[512,32]{0,1:T(8,128)S(1)}, f32[512,32]{0,1:T(8,128)}, u32[]{:S(2)}) copy-start(f32[512,32]{0,1:T(8,128)} %copy-done.9) | copy-start | bytes 196612
  420.5 4.4 copy-start.5
  420.9 15.1 %copy-start.7 = (f32[512,512]{1,0:T(8,128)}, f32[512,512]{1,0:T(8,128)S(1)}, u32[]{:S(2)}) copy-start(f32[512,512]{1,0:T(8,128)S(1)} %fusion.63) | copy-start | bytes 3145732
  439.9 1.8 copy-start.6
  439.9 2.0 copy-start.8
  440.0 2.0 copy-start.11
  442.0 62.6 %copy-start.1 = (f32[512,32]{0,1:T(8,128)S(1)}, f32[512,32]{0,1:T(8,128)}, u32[]{:S(2)}) copy-start(f32[512,32]{0,1:T(8,128)} %param.14) | copy-start | bytes 196612
Sparse Core Ops, SparseCore 0:
  73.1 110.8 all-gather.5
  186.1 110.8 all-gather.7
  420.6 81.3 reduce-scatter.1

commit v2 on v1

v2 whole, which is shorter than its diff:
```python
import functools
import jax
import jax.numpy as jnp
from jax import lax
from jax.experimental import pallas as pl
from jax.experimental.pallas import tpu as pltpu
from jax.sharding import PartitionSpec as P

MESH = pl.DeviceIdType.MESH
MB = 1 << 20
F32, BF16 = jnp.float32, jnp.bfloat16


def dot(a, b, ca=1, cb=0):
    return lax.dot_general(a, b, (((ca,), (cb,)), ((), ())), preferred_element_type=F32)


def iota(shape, dim):
    return lax.broadcasted_iota(jnp.int32, shape, dim)


def loop(low, high, body):
    def one(n, carry):
        body(n)
        return carry

    lax.fori_loop(low, high, one, 0)


def gather_plan():
    plan = {}
    for da in (0, 1, -1, 2):
        if da:
            for q in (0, 1) if abs(da) == 2 else (None,):
                plan[("a", da, 0, q)] = len(plan)
        for db in (1, -1):
            plan[("b", da, db, None)] = len(plan)
        for q in (0, 1):
            plan[("b", da, 2, q)] = len(plan)
    return plan


PLAN = gather_plan()


def power_of_two(n):
    size = jnp.abs(n)
    up, down = jnp.ones(n.shape, F32), jnp.ones(n.shape, F32)
    for b in range(7):
        bit = ((size >> b) & 1) == 1
        up = jnp.where(bit, up * (2.0 ** (1 << b)), up)
        down = jnp.where(bit, down * (2.0 ** -(1 << b)), down)
    return jnp.where(n >= 0, up, down)


def kernel(
    lens, logd, hid, w, xin, dyin,
    y_out, dx_out, gm_out, exp_out,
    hbuf, wbuf, acc, bc, x, dy, xs, dys, xst, dyst, xe, de, yacc, dxacc,
    run3, runt, ent2, end2, mid2, cnt, msk, dgd, dg10, dgb, gd, gdt, g10, g10t,
    ssend, gsend, frecv, grecv, sin, rsum, dtile, drecv,
    s1, f1, s2, f2, top, box,
    lsem, asend, arecv, tsend, trecv, rsend, rrecv, msend, mrecv,
):
    i = lax.axis_index("seq")
    j = lax.axis_index("mp")
    px, py = i // 4, lax.rem(i, 4)

    def owner(half, da, db):
        dx = half * da + (1 - half) * db
        dyy = half * db + (1 - half) * da
        return lax.rem(px + dx + 4, 4) * 4 + lax.rem(py + dyy + 4, 4)

    def device(half, axis, sign):
        return (owner(half, sign, 0) if axis == "a" else owner(half, 0, sign), j)

    def remote(src, dst, send_sem, recv_sem, dev):
        return pltpu.make_async_remote_copy(
            src_ref=src, dst_ref=dst, send_sem=send_sem, recv_sem=recv_sem,
            device_id=dev, device_id_type=MESH,
        )

    loads = [
        pltpu.make_async_copy(src, dst, lsem.at[n])
        for n, (src, dst) in enumerate(((xin, x), (dyin, dy), (w, wbuf.at[i]), (hid, hbuf)))
    ]
    for c in loads:
        c.start()
    barrier = pltpu.get_barrier_semaphore()
    for d in range(1, 16):
        pl.semaphore_signal(barrier, inc=1, device_id=(lax.rem(i + d, 16), j), device_id_type=MESH)
    for d in range(1, 8):
        pl.semaphore_signal(barrier, inc=1, device_id=(i, lax.rem(j + d, 8)), device_id_type=MESH)
    pl.semaphore_wait(barrier, 22)

    def rows(half, q):
        return pl.ds(256 * half, 256) if q is None else pl.ds(256 * half + 128 * q, 128)

    sent = []

    def send(half, axis, da, db, q, sign):
        m = PLAN[(axis, da, db, q)]
        if axis == "a":
            oa, ob = (da + sign if abs(da) == 1 else -sign), 0
        else:
            oa, ob = da, (0 if abs(db) == 1 else -sign)
        k = owner(half, oa, ob)
        src = w if (oa, ob) == (0, 0) else wbuf.at[k]
        c = remote(
            src.at[rows(half, q), :], wbuf.at[k, rows(half, q), :],
            asend.at[half, m], arecv.at[half, m], device(half, axis, sign),
        )
        c.start()
        sent.append(c)

    def got(half, axis, da, db, q):
        m = PLAN[(axis, da, db, q)]
        ref = wbuf.at[owner(half, da, db), rows(half, q), :]
        remote(ref, ref, asend.at[half, m], arecv.at[half, m], device(half, axis, 1)).wait_recv()

    def out_b(half, da):
        send(half, "b", da, -1, None, 1)
        send(half, "b", da, 1, None, -1)

    def fwd_b(half, da):
        got(half, "b", da, -1, None)
        send(half, "b", da, 2, 0, 1)
        got(half, "b", da, 1, None)
        send(half, "b", da, 2, 1, -1)

    def mul(pairs):
        def one(n):
            half, r = lax.rem(n, 2), n // 2
            da = sum(jnp.where(r == t, p[0], 0) for t, p in enumerate(pairs))
            db = sum(jnp.where(r == t, p[1], 0) for t, p in enumerate(pairs))
            k = owner(half, da, db)
            off = pl.multiple_of(half * 256, 256)
            cols = pl.ds(pl.multiple_of(k * 512 + off, 256), 256)
            acc[...] += dot(hbuf[:, cols], wbuf[k, pl.ds(off, 256), :])

        loop(0, 2 * len(pairs), one)

    def tables():
        tri = (iota((512, 512), 0) >= iota((512, 512), 1)).astype(F32).astype(BF16)

        def split(v, parts):
            out = []
            for _ in range(parts):
                top_part = v.astype(BF16)
                out.append(top_part)
                v = v - top_part.astype(F32)
            return out

        run = sum(dot(tri, p) for p in split(logd[...], 3))
        none = jnp.zeros((512, 32), F32)
        run3[...] = jnp.concatenate([p.astype(F32) for p in split(run, 3)] + [none], axis=1).astype(BF16)
        runt[...] = jnp.concatenate([run, none, none, none], axis=1).T

        first = i * 512
        begin = jnp.int32(0)
        t_col, t_row = iota((512, 128), 0), iota((8, 512), 1)
        c_col, c_row = jnp.zeros((512, 128), jnp.int32), jnp.zeros((8, 512), jnp.int32)
        c_mid, c_end = jnp.int32(0), jnp.int32(0)
        for d in range(8):
            at = begin - first
            inside = jnp.where(at >= 0, 1, 0)
            c_col += jnp.where(t_col >= at, inside, 0)
            c_row += jnp.where(t_row >= at, inside, 0)
            c_mid += jnp.where(at <= 255, inside, 0)
            c_end += jnp.where(at <= 511, inside, 0)
            begin = begin + lens[d]
        cnt[0:8, :] = c_row.astype(F32)
        col, row = c_col[:, 0:1], c_row[0:1, :]
        same = jnp.where(col == row, 1.0, 0.0)
        msk[...] = jnp.where(iota((512, 512), 0) >= iota((512, 512), 1), same, 0.0)
        seg = c_col[:, 0:32]
        ent = jnp.where(seg == 0, jnp.exp(run), 0.0)
        end = jnp.where(seg == c_end, jnp.exp(jnp.minimum(run[511:512, :] - run, 0.0)), 0.0)
        mid = jnp.where(seg == c_mid, jnp.exp(-jnp.abs(run - run[255:256, :])), 0.0)
        for ref, v in ((ent2, ent), (end2, end), (mid2, mid)):
            ref[...] = jnp.concatenate([p.astype(F32) for p in split(v, 2)] + [none, none], axis=1).astype(BF16)
        return jnp.where(c_end == 0, 1.0, 0.0)

    def spread(first_head, width, parts):
        r, c = iota((128, 256), 0), iota((128, 256), 1)
        hit = ((r & 31) == first_head + c // width) & (r < 32 * parts)
        return jnp.where(hit, 1.0, 0.0).astype(BF16)

    def scaled(c):
        cols = pl.ds(pl.multiple_of(256 * c, 256), 256)
        oh = spread(4 * c, 64, 2)
        a = (dy[:, cols].astype(F32) * dot(ent2[...], oh)).astype(BF16)
        dys[:, cols] = a
        dyst[cols, :] = a.T
        b = (x[:, cols].astype(F32) * dot(end2[...], oh)).astype(BF16)
        xs[:, cols] = b
        xst[cols, :] = b.T
        m = dot(mid2[...], oh)
        p = (x[0:256, cols].astype(F32) * m[0:256]).astype(BF16)
        q = (dy[256:512, cols].astype(F32) * m[256:512]).astype(BF16)
        xe[:, cols] = p
        de[:, cols] = q
        dg10[...] += dot(q, p, 1, 1)

    def weights(r, hp, b, e):
        rb = r[256 * b : 256 * b + 256, 128 * e : 128 * e + 128]
        rt = runt[pl.ds(2 * hp + e, 1), 256 * b : 256 * b + 256]
        return jnp.concatenate([rb, rb], axis=1) - rt

    def one_head(v, e):
        return jnp.where((iota(v.shape, 1) // 64) == e, v, jnp.zeros_like(v))

    def dgram_pair(hp):
        r = dot(run3[...], spread(2 * hp, 128, 3))
        cols = pl.ds(pl.multiple_of(128 * hp, 128), 128)
        for b in (0, 1):
            rs = slice(256 * b, 256 * b + 256)
            dyp, xp = dy[rs, cols], x[rs, cols]
            total = dgd[b]
            for e in (0, 1):
                s = dot(dyp, one_head(xp, e), 1, 1)
                total += s * jnp.exp(jnp.minimum(weights(r, hp, b, e), 0.0))
            dgd[b] = total
        tail = jnp.exp(r[504:512, :])
        dtile[hp, 0:1, :] = tail[7:8, 0:128] * whole
        dtile[hp, 1:2, :] = tail[7:8, 128:256] * whole

    def send_decays():
        drecv[i] = dtile[i]

        def one(d):
            q = lax.rem(i + d, 16)
            remote(dtile.at[q], drecv.at[i], tsend.at[4, q], trecv.at[4, i], (q, j)).start()

        loop(1, 16, one)

    for half in (0, 1):
        send(half, "a", -1, 0, None, 1)
        send(half, "a", 1, 0, None, -1)
    for half in (0, 1):
        out_b(half, 0)
    acc[...] = jnp.zeros_like(acc)
    dg10[...] = jnp.zeros_like(dg10)
    dgd[...] = jnp.zeros_like(dgd)
    dtile[...] = jnp.zeros_like(dtile)
    whole = tables()
    loads[0].wait()
    loads[1].wait()
    for half in (0, 1):
        got(half, "a", -1, 0, None)
        send(half, "a", 2, 0, 0, 1)
        got(half, "a", 1, 0, None)
        send(half, "a", 2, 0, 1, -1)
    for half in (0, 1):
        out_b(half, -1)
        out_b(half, 1)
    loads[2].wait()
    loads[3].wait()
    mul([(0, 0)])
    loop(0, 4, dgram_pair)
    for half in (0, 1):
        fwd_b(half, 0)
    mul([(-1, 0), (1, 0)])
    for half in (0, 1):
        got(half, "a", 2, 0, 0)
        got(half, "a", 2, 0, 1)
        out_b(half, 2)
    loop(4, 8, dgram_pair)
    mul([(0, -1), (0, 1), (2, 0)])
    for half in (0, 1):
        fwd_b(half, -1)
        fwd_b(half, 1)
    loop(8, 16, dgram_pair)
    send_decays()
    mul([(-1, -1), (-1, 1), (1, -1), (1, 1)])
    for half in (0, 1):
        fwd_b(half, 2)
    loop(0, 8, scaled)
    dgb[0:256, 0:256] = (dgd[0] * msk[0:256, 0:256]).astype(BF16)
    dgb[256:512, 256:512] = (dgd[1] * msk[256:512, 256:512]).astype(BF16)
    dgb[256:512, 0:256] = (dg10[...] * msk[256:512, 0:256]).astype(BF16)
    dgb[0:256, 256:512] = jnp.zeros((256, 256), BF16)
    mul([(2, -1), (2, 1)])
    for da in (0, -1, 1, 2):
        for half in (0, 1):
            got(half, "b", da, 2, 0)
            got(half, "b", da, 2, 1)
        mul([(da, 2)])
    bc[...] = acc[...].astype(BF16)

    def pair_rows(q):
        return pl.ds(pl.multiple_of(128 * q, 128), 128)

    def states(kind, left, cols, out, into):
        def one(d):
            q = lax.rem(i + d, 16)
            out[q] = dot(left[pair_rows(q), :], bc[:, cols]).astype(BF16)
            remote(out.at[q], into.at[i], tsend.at[kind, q], trecv.at[kind, i], (q, j)).start()

        loop(1, 16, one)
        into[i] = dot(left[pair_rows(i), :], bc[:, cols]).astype(BF16)

    def wait_in(kind, into):
        def one(d):
            k = lax.rem(i + d, 16)
            remote(into.at[k], into.at[k], tsend.at[kind, k], trecv.at[kind, k], (k, j)).wait_recv()

        loop(1, 16, one)

    def wait_out(kind, src):
        def one(d):
            k = lax.rem(i + d, 16)
            remote(src.at[k], src.at[k], tsend.at[kind, k], trecv.at[kind, k], (k, j)).wait_send()

        loop(1, 16, one)

    def scan(kind, into, out, back, backward):
        def one(n, state):
            k = 15 - n if backward else n
            out[k] = state.astype(BF16)
            d = drecv[k]
            d0 = jnp.concatenate([d[0:1, :], d[0:1, :]], axis=1)
            d1 = jnp.concatenate([d[1:2, :], d[1:2, :]], axis=1)
            new = into[k].astype(F32)
            return jnp.concatenate([state[0:64] * d0 + new[0:64], state[64:128] * d1 + new[64:128]], axis=0)

        lax.fori_loop(0, 16, one, jnp.zeros((128, 256), F32))

        def ship(d):
            k = lax.rem(i + d, 16)
            remote(out.at[k], back.at[i], tsend.at[kind, k], trecv.at[kind, i], (k, j)).start()

        loop(1, 16, ship)
        back[i] = out[i]

    def intra_pair(hp):
        r = dot(run3[...], spread(2 * hp, 128, 3))
        cols = pl.ds(pl.multiple_of(128 * hp, 128), 128)
        for b in (0, 1):
            rs = slice(256 * b, 256 * b + 256)
            dyp, xp = dy[rs, cols], x[rs, cols]
            ya = jnp.zeros((256, 128), F32)
            da = jnp.zeros((256, 128), F32)
            for e in (0, 1):
                diff = weights(r, hp, b, e)
                mix = (gd[b] * jnp.exp(jnp.minimum(diff, 0.0))).astype(BF16)
                ya += dot(mix, one_head(xp, e))
                mixt = (gdt[b] * jnp.exp(jnp.minimum(-diff, 0.0))).astype(BF16)
                da += dot(mixt, one_head(dyp, e))
            yacc[rs, cols] = ya
            dxacc[rs, cols] = da

    def across(c):
        cols = pl.ds(pl.multiple_of(256 * c, 256), 256)
        m = dot(mid2[...], spread(4 * c, 64, 2))
        yacc[256:512, cols] += m[256:512] * dot(g10[...], xe[:, cols])
        dxacc[0:256, cols] += m[0:256] * dot(g10t[...], de[:, cols])

    states(0, xst, slice(0, 256), ssend, frecv)
    states(1, dyst, slice(256, 512), gsend, grecv)
    b_map, c_map = bc[:, 0:256], bc[:, 256:512]
    row = cnt[0:1, :]
    for b in (0, 1):
        rs = slice(256 * b, 256 * b + 256)
        gd[b] = dot(c_map[rs], b_map[rs], 1, 1) * msk[rs, rs]
        gdt[b] = dot(b_map[rs], c_map[rs], 1, 1) * msk[rs, rs].T
    g10[...] = (dot(c_map[256:512], b_map[0:256], 1, 1) * msk[256:512, 0:256]).astype(BF16)
    g10t[...] = (dot(b_map[0:256], c_map[256:512], 1, 1) * msk[256:512, 0:256].T).astype(BF16)
    acc[:, 0:256] = dot(dgb[...], c_map, 0, 0)
    acc[:, 256:512] = dot(dgb[...], b_map)
    loop(0, 6, intra_pair)
    wait_in(4, drecv)
    wait_in(0, frecv)
    wait_out(0, ssend)
    scan(2, frecv, ssend, sin, False)
    loop(6, 10, intra_pair)
    wait_in(1, grecv)
    wait_out(1, gsend)
    scan(3, grecv, gsend, rsum, True)
    loop(10, 16, intra_pair)
    loop(0, 8, across)
    wait_in(2, sin)
    acc[:, 256:512] += sum(dot(dys[:, 128 * q : 128 * q + 128], sin[q]) for q in range(16))
    wait_in(3, rsum)
    acc[:, 0:256] += sum(dot(xs[:, 128 * q : 128 * q + 128], rsum[q]) for q in range(16))
    bc2 = acc[...].T.astype(BF16)
    dgb[...] = bc2
    for c in sent:
        c.wait_send()

    top[...] = jnp.zeros_like(top)

    def block(k):
        cols = pl.ds(pl.multiple_of(512 * k, 512), 512)
        p = dot(dgb[...], hbuf[:, cols])
        top[...] = jnp.maximum(top[...], jnp.max(jnp.abs(p).reshape(64, 8, 512), axis=0))
        wbuf[k] = p.astype(BF16)

    loop(0, 16, block)
    largest = jnp.max(top[...])
    box[0] = jnp.full((8, 128), largest, F32)

    def spread_max(kind, count, dev):
        base = 16 * kind

        def ship(d):
            remote(box.at[0], box.at[base + d], msend.at[base + d], mrecv.at[base + d], dev(d)).start()

        def wait(d):
            remote(box.at[0], box.at[base + d], msend.at[base + d], mrecv.at[base + d], dev(d)).wait()

        loop(1, count, ship)
        loop(1, count, wait)
        best = box[0]
        for d in range(1, count):
            best = jnp.maximum(best, box[base + d])
        return best

    box[0] = spread_max(0, 16, lambda d: (lax.rem(i + d, 16), j))
    best = spread_max(1, 8, lambda d: (i, lax.rem(j + d, 8)))
    guess = jnp.ceil(jnp.log2(best)).astype(jnp.int32)
    guess = jnp.where(power_of_two(guess) < best, guess + 1, guess)
    guess = jnp.where(power_of_two(guess - 1) >= best, guess - 1, guess)
    exp_out[...] = guess.astype(F32)
    scale = jnp.max(power_of_two(20 - guess))

    def part_of(n):
        return lax.rem(6 - n // 2, 4), lax.rem(n, 2)

    def half_rows(half, at, size):
        return pl.ds(pl.multiple_of(256 * half + at, 128), size)

    def quant(k, rs):
        return jnp.floor(wbuf[k, rs, :].astype(F32) * scale + 0.5)

    def msg(n, t, src, dst, axis, sign, half):
        return remote(src, dst, rsend.at[n, t], rrecv.at[n, t], device(half, axis, sign))

    def stage0(n):
        da, half = part_of(n)
        k = owner(half, da, 2)
        rs = half_rows(half, 0, 256)
        wbuf[k, rs, :] = quant(k, rs).astype(BF16)
        msg(n, 0, wbuf.at[k, half_rows(half, 0, 128), :], s1.at[n, 0], "b", 1, half).start()
        msg(n, 1, wbuf.at[k, half_rows(half, 128, 128), :], s1.at[n, 1], "b", -1, half).start()

    def stage1(n):
        da, half = part_of(n)
        for t, sign in ((0, 1), (1, -1)):
            k = owner(half, da, sign)
            with_sum = half_rows(half, 128 * t, 128)
            alone = half_rows(half, 128 - 128 * t, 128)
            wbuf[k, alone, :] = quant(k, alone).astype(BF16)
            own = quant(k, with_sum)
            msg(n, t, s1.at[n, t], s1.at[n, t], "b", 1, half).wait_recv()
            wbuf[k, with_sum, :] = (own + s1[n, t].astype(F32)).astype(BF16)
            msg(n, 2 + t, wbuf.at[k, half_rows(half, 0, 256), :], f1.at[n, t], "b", sign, half).start()

    def total1(n):
        da, half = part_of(n)
        rs = half_rows(half, 0, 256)
        k = owner(half, da, 0)
        own = quant(k, rs)
        for t in (0, 1):
            msg(n, 2 + t, f1.at[n, t], f1.at[n, t], "b", 1, half).wait_recv()
        return k, rs, own + f1[n, 0].astype(F32) + f1[n, 1].astype(F32)

    def stage2(n):
        k, rs, total = total1(n)
        wbuf[k, rs, :] = total.astype(BF16)

    def finish_y(c):
        cols = pl.ds(pl.multiple_of(256 * c, 256), 256)
        oh = spread(4 * c, 64, 2)
        c_map, b_map = bc[:, 256:512], bc[:, 0:256]
        for t in (0, 1):
            at = pl.ds(pl.multiple_of(256 * c + 128 * t, 128), 128)
            hs = slice(128 * t, 128 * t + 128)
            carry = dot(c_map, sin[2 * c + t], 1, 1) * dot(ent2[...], oh[:, hs])
            hbuf[:, at] = (yacc[:, at] + carry).astype(BF16)
            carry = dot(b_map, rsum[2 * c + t], 1, 1) * dot(end2[...], oh[:, hs])
            hbuf[:, pl.ds(pl.multiple_of(2048 + 256 * c + 128 * t, 128), 128)] = (dxacc[:, at] + carry).astype(BF16)

    loop(0, 8, stage0)
    loop(0, 8, finish_y)
    ends = [
        pltpu.make_async_copy(hbuf.at[:, 0:2048], y_out, lsem.at[0]),
        pltpu.make_async_copy(hbuf.at[:, 2048:4096], dx_out, lsem.at[1]),
    ]
    for c in ends:
        c.start()
    loop(0, 8, stage1)
    loop(0, 2, stage2)

    def stage3(half):
        k = owner(half, 2, 0)
        msg(8 + half, 0, wbuf.at[k, half_rows(half, 0, 128), :], s2.at[half, 0], "a", 1, half).start()
        msg(8 + half, 1, wbuf.at[k, half_rows(half, 128, 128), :], s2.at[half, 1], "a", -1, half).start()

    loop(0, 2, stage3)
    loop(2, 4, stage2)
    loop(6, 8, stage2)

    def stage4(half):
        for t, sign in ((0, 1), (1, -1)):
            k = owner(half, sign, 0)
            rs = half_rows(half, 128 * t, 128)
            msg(8 + half, t, s2.at[half, t], s2.at[half, t], "a", 1, half).wait_recv()
            wbuf[k, rs, :] = (wbuf[k, rs, :].astype(F32) + s2[half, t].astype(F32)).astype(BF16)
            msg(8 + half, 2 + t, wbuf.at[k, half_rows(half, 0, 256), :], f2.at[half, t], "a", sign, half).start()

    loop(0, 2, stage4)

    def stage5(n):
        _, rs, total = total1(n)
        acc[rs, :] = total

    loop(4, 6, stage5)
    for half in (0, 1):
        for t in (0, 1):
            msg(8 + half, 2 + t, f2.at[half, t], f2.at[half, t], "a", 1, half).wait_recv()
        rs = slice(256 * half, 256 * half + 256)
        total = acc[rs, :] + f2[half, 0].astype(F32) + f2[half, 1].astype(F32)
        gm_out[:, rs] = (total * 2.0 ** -20).T

    for kind, src in ((2, ssend), (3, gsend), (4, dtile)):
        wait_out(kind, src)

    def left(n):
        for t in (0, 1):
            msg(n, t, s1.at[0, 0], s1.at[0, 0], "b", 1, 0).wait_send()
            msg(n, 2 + t, f1.at[0, 0], f1.at[0, 0], "b", 1, 0).wait_send()

    loop(0, 10, left)
    for c in ends:
        c.wait()


def mixer(lengths, hidden, w, x, log_decay, dy):
    n = len(PLAN)
    vm = pltpu.VMEM
    anyw = pl.BlockSpec(memory_space=pl.ANY)
    vspec = pl.BlockSpec(memory_space=pltpu.VMEM)
    scratch = [
        vm((512, 8192), BF16), vm((16, 512, 512), BF16), vm((512, 512), F32), vm((512, 512), BF16),
        vm((512, 2048), BF16), vm((512, 2048), BF16), vm((512, 2048), BF16), vm((512, 2048), BF16),
        vm((2048, 512), BF16), vm((2048, 512), BF16), vm((256, 2048), BF16), vm((256, 2048), BF16),
        vm((512, 2048), F32), vm((512, 2048), F32),
        vm((512, 128), BF16), vm((128, 512), F32), vm((512, 128), BF16), vm((512, 128), BF16), vm((512, 128), BF16),
        vm((8, 512), F32), vm((512, 512), F32), vm((2, 256, 256), F32), vm((256, 256), F32), vm((512, 512), BF16),
        vm((2, 256, 256), F32), vm((2, 256, 256), F32), vm((256, 256), BF16), vm((256, 256), BF16),
        vm((16, 128, 256), BF16), vm((16, 128, 256), BF16), vm((16, 128, 256), BF16), vm((16, 128, 256), BF16),
        vm((16, 128, 256), BF16), vm((16, 128, 256), BF16),
        vm((16, 8, 128), F32), vm((16, 8, 128), F32),
        vm((8, 2, 128, 512), BF16), vm((8, 2, 256, 512), BF16), vm((2, 2, 128, 512), BF16), vm((2, 2, 256, 512), BF16),
        vm((8, 512), F32), vm((32, 8, 128), F32),
        pltpu.SemaphoreType.DMA((4,)), pltpu.SemaphoreType.DMA((2, n)), pltpu.SemaphoreType.DMA((2, n)),
        pltpu.SemaphoreType.DMA((5, 16)), pltpu.SemaphoreType.DMA((5, 16)),
        pltpu.SemaphoreType.DMA((10, 4)), pltpu.SemaphoreType.DMA((10, 4)),
        pltpu.SemaphoreType.DMA((32,)), pltpu.SemaphoreType.DMA((32,)),
    ]
    y, dx, gm, ex = pl.pallas_call(
        kernel,
        out_shape=(
            jax.ShapeDtypeStruct((512, 2048), BF16), jax.ShapeDtypeStruct((512, 2048), BF16),
            jax.ShapeDtypeStruct((512, 512), F32), jax.ShapeDtypeStruct((8, 128), F32),
        ),
        in_specs=[pl.BlockSpec(memory_space=pltpu.SMEM), vspec, anyw, anyw, anyw, anyw],
        out_specs=(anyw, anyw, vspec, vspec),
        scratch_shapes=scratch,
        compiler_params=pltpu.CompilerParams(collective_id=0, has_side_effects=True, vmem_limit_bytes=63 * MB),
        name="mixer",
    )(lengths, log_decay, hidden, w, x, dy)
    return y, dx, gm, ex[0, 0]


def solution(mesh):
    in_specs = (P(), P("seq", None), P("seq", "mp"), P("seq", "mp"), P("seq", "mp"), P("seq", "mp"))
    out_specs = (P("seq", "mp"), P("seq", "mp"), P("seq", "mp"), P())
    return jax.shard_map(mixer, mesh=mesh, in_specs=in_specs, out_specs=out_specs, check_vma=False)
```

time: 521 us -> 190 us (0.36); the launches traced: 513 us -> 190 us
  waiting for transfers between devices: 221 us -> 0 us
  Pallas kernels: 52 us -> 180 us
  blocking collectives: 93.8 us -> 0 us
  matrix products: 70 us -> 0 us
  other arithmetic: 39.7 us -> 0 us
  between operations: 16.4 us -> 0.64 us
  local copies, waits for them, and re-layouts: 18.7 us -> 9.11 us
    all_gather x2 -> x0, waiting for transfers between devices: 172 us -> none  [prefix(): lax.all_gather(a.astype(kind), axis)]
    pallas_call x1, Pallas kernels: 52 us -> 180 us  [mixer(): pl.pallas_call(kernel, out_shape=(jax.ShapeDtypeStruct((512, 2048), BF16)...]
    dot_general x13 -> x0, matrix products: 70 us -> none  [the longest x1 12.2 us: shards(): jnp.einsum('td,tc->dc', hidden_in, dproj, preferred_element_type=jnp.floa...]
    pmax x1 -> x0, blocking collectives: 64.8 us -> none  [quantized(): largest = lax.pmax(jnp.max(jnp.abs(incomplete_figure)), ('seq', 'mp'))]
    reduce_scatter x1 -> x0, waiting for transfers between devices: 49 us -> none  [shards(): lax.psum_scatter(fixed.astype(jnp.bfloat16), 'seq', scatter_dimension=0,...]
    all_gather x1 -> x0, blocking collectives: 29 us -> none  [prefix(): lax.all_gather(a.astype(kind), axis)]
    add x16 -> x0, other arithmetic: 24.6 us -> none  [the longest x15 24.6 us: link_states(): later[0][:, :, None, None] * earlier[1] + later[1]]
    convert_element_type x18 -> x0, other arithmetic: 9.75 us -> none  [the longest x1 9.54 us: shards(): fixed.astype(jnp.bfloat16)]
  transfers between devices with their start and end apart: 3 -> 0, of which waited for: 3 -> 0; matrix products, arithmetic and copies ran while one was open for 11% -> 0% of each run, Pallas kernels for 0% -> 0%
where the time goes in v2:
time: 190 us
  Pallas kernels  180 us (95%)
  local copies, waits for them, and re-layouts  9.11 us (5%)
    pallas_call x1, Pallas kernels, mixer(): pl.pallas_call(kernel, out_shape=(jax.ShapeDtypeStruct((512, 2048), BF16)...  180 us
    unnamed x8, local copies, waits for them, and re-layouts  7.91 us

profile of v2, /device:TPU:0, one launch (start us, length us, event | category | flops | bytes accessed | tf_op | source)
XLA Modules:
  0.0 189.6 jit_solution(11863257730404698044)
XLA Ops:
  0.6 1.7 copy.10.logd
  2.3 179.9 %mixer.1 = (bf16[512,2048]{1,0:T(8,128)(2,1)}, bf16[512,2048]{1,0:T(8,128)(2,1)}, f32[512,512]{1,0:T(8,128)}, f32[8,128]{1,0:T(8,128)}) custom-call(s32[8]{0:T(128)} %lens.1, f32[512,32]{1,0:T(8,128)} %copy.10.logd, bf16[512,8192]{1,0:T(8,128)(2,1)} %hid.1, bf16[512,512]{1,0:T(8,128)(2,1)} %w.1, bf16[512,2048]{1,0:T(8,128)(2,1)} %xin.1, bf16[512,2048]{1,0:T(8,128)(2,1)} %dyin.1), custom_call_target="tpu_custom_call" | custom-call | tf_op jit(solution)/shard_map/mixer/pallas_call | solution.py:562
  182.2 1.2 slice.3
  183.4 0.0 copy-start
  183.4 3.3 %copy.14 = bf16[512,2048]{1,0:T(8,128)(2,1)} copy(bf16[512,2048]{1,0:T(8,128)(2,1)} %get-tuple-element.16) | data formatting | bytes 4194304
  186.7 0.0 copy-done
  186.7 0.0 copy-start.1
  186.7 1.3 copy.15
  188.0 0.6 copy-done.1
  188.7 1.0 copy.16
Async XLA Ops:
  183.4 3.3 %copy-start = (bf16[512,2048]{1,0:T(8,128)(2,1)S(1)}, bf16[512,2048]{1,0:T(8,128)(2,1)}, u32[]{:S(2)}) copy-start(bf16[512,2048]{1,0:T(8,128)(2,1)} %get-tuple-element.17) | copy-start | bytes 6291460
  186.7 2.0 %copy-start.1 = (f32[512,512]{1,0:T(8,128)S(1)}, f32[512,512]{1,0:T(8,128)}, u32[]{:S(2)}) copy-start(f32[512,512]{1,0:T(8,128)} %get-tuple-element.18) | copy-start | bytes 3145732

commit v3 on v2

v3 whole, which is shorter than its diff:
```python
import functools
import jax
import jax.numpy as jnp
from jax import lax
from jax.experimental import pallas as pl
from jax.experimental.pallas import tpu as pltpu
from jax.sharding import PartitionSpec as P

MESH = pl.DeviceIdType.MESH
MB = 1 << 20
F32, BF16 = jnp.float32, jnp.bfloat16


def dot(a, b, ca=1, cb=0):
    return lax.dot_general(a, b, (((ca,), (cb,)), ((), ())), preferred_element_type=F32)


def iota(shape, dim):
    return lax.broadcasted_iota(jnp.int32, shape, dim)


def loop(low, high, body):
    def one(n, carry):
        body(n)
        return carry

    lax.fori_loop(low, high, one, 0)


def gather_plan():
    plan = {}
    for da in (0, 1, -1, 2):
        if da:
            for q in (0, 1) if abs(da) == 2 else (None,):
                plan[("a", da, 0, q)] = len(plan)
        for db in (1, -1):
            plan[("b", da, db, None)] = len(plan)
        for q in (0, 1):
            plan[("b", da, 2, q)] = len(plan)
    return plan


PLAN = gather_plan()


def power_of_two(n):
    size = jnp.abs(n)
    up, down = jnp.ones(n.shape, F32), jnp.ones(n.shape, F32)
    for b in range(7):
        bit = ((size >> b) & 1) == 1
        up = jnp.where(bit, up * (2.0 ** (1 << b)), up)
        down = jnp.where(bit, down * (2.0 ** -(1 << b)), down)
    return jnp.where(n >= 0, up, down)


def kernel(
    lens, logd, hid, w, xin, dyin,
    y_out, dx_out, gm_out, exp_out,
    ldv, hbuf, wbuf, acc, bc, x, dy, xs, dys, xst, dyst, xe, de, yacc, dxacc,
    run3, runt, ent2, end2, mid2, cnt, msk, dgd, dg10, dgb, gd, gdt, g10, g10t,
    ssend, gsend, frecv, grecv, sin, rsum, dtile, drecv,
    s1, f1, s2, f2, top, box,
    lsem, asend, arecv, tsend, trecv, rsend, rrecv, msend, mrecv,
):
    i = lax.axis_index("seq")
    j = lax.axis_index("mp")
    px, py = i // 4, lax.rem(i, 4)

    def owner(half, da, db):
        dx = half * da + (1 - half) * db
        dyy = half * db + (1 - half) * da
        return lax.rem(px + dx + 4, 4) * 4 + lax.rem(py + dyy + 4, 4)

    def device(half, axis, sign):
        return (owner(half, sign, 0) if axis == "a" else owner(half, 0, sign), j)

    def remote(src, dst, send_sem, recv_sem, dev):
        return pltpu.make_async_remote_copy(
            src_ref=src, dst_ref=dst, send_sem=send_sem, recv_sem=recv_sem,
            device_id=dev, device_id_type=MESH,
        )

    own = [
        (w.at[256 * h : 256 * h + 256, 256 * p : 256 * p + 256], wbuf.at[i, p, h]) for p in (0, 1) for h in (0, 1)
    ]
    loads = [
        pltpu.make_async_copy(src, dst, lsem.at[n])
        for n, (src, dst) in enumerate(own + [(logd, ldv), (xin, x), (dyin, dy), (hid, hbuf)])
    ]
    for c in loads:
        c.start()
    barrier = pltpu.get_barrier_semaphore()
    for d in range(1, 16):
        pl.semaphore_signal(barrier, inc=1, device_id=(lax.rem(i + d, 16), j), device_id_type=MESH)
    for d in range(1, 8):
        pl.semaphore_signal(barrier, inc=1, device_id=(i, lax.rem(j + d, 8)), device_id_type=MESH)
    pl.semaphore_wait(barrier, 22)

    def rows(q):
        return pl.ds(0, 256) if q is None else pl.ds(128 * q, 128)

    sent = []

    def send(part, half, axis, da, db, q, sign):
        m = PLAN[(axis, da, db, q)]
        if axis == "a":
            oa, ob = (da + sign if abs(da) == 1 else -sign), 0
        else:
            oa, ob = da, (0 if abs(db) == 1 else -sign)
        k = owner(half, oa, ob)
        piece = wbuf.at[k, part, half, rows(q), :]
        c = remote(
            piece, piece,
            asend.at[part, half, m], arecv.at[part, half, m], device(half, axis, sign),
        )
        c.start()
        sent.append(c)

    def got(part, half, axis, da, db, q):
        m = PLAN[(axis, da, db, q)]
        ref = wbuf.at[owner(half, da, db), part, half, rows(q), :]
        remote(ref, ref, asend.at[part, half, m], arecv.at[part, half, m], device(half, axis, 1)).wait_recv()

    def out_b(part, half, da):
        send(part, half, "b", da, -1, None, 1)
        send(part, half, "b", da, 1, None, -1)

    def fwd_b(part, das):
        for da in das:
            for half in (0, 1):
                got(part, half, "b", da, -1, None)
                send(part, half, "b", da, 2, 0, 1)
                got(part, half, "b", da, 1, None)
                send(part, half, "b", da, 2, 1, -1)

    def step0(part):
        for half in (0, 1):
            send(part, half, "a", -1, 0, None, 1)
            send(part, half, "a", 1, 0, None, -1)
        for half in (0, 1):
            out_b(part, half, 0)

    def step1(part):
        for half in (0, 1):
            got(part, half, "a", -1, 0, None)
            send(part, half, "a", 2, 0, 0, 1)
            got(part, half, "a", 1, 0, None)
            send(part, half, "a", 2, 0, 1, -1)
        for half in (0, 1):
            out_b(part, half, -1)
            out_b(part, half, 1)

    def step3(part):
        for half in (0, 1):
            got(part, half, "a", 2, 0, 0)
            got(part, half, "a", 2, 0, 1)
            out_b(part, half, 2)

    def last(part, das):
        for da in das:
            for half in (0, 1):
                got(part, half, "b", da, 2, 0)
                got(part, half, "b", da, 2, 1)

    def mul(part, pairs):
        def one(n):
            half, r = lax.rem(n, 2), n // 2
            da = sum(jnp.where(r == t, p[0], 0) for t, p in enumerate(pairs))
            db = sum(jnp.where(r == t, p[1], 0) for t, p in enumerate(pairs))
            k = owner(half, da, db)
            off = pl.multiple_of(half * 256, 256)
            cols = pl.ds(pl.multiple_of(k * 512 + off, 256), 256)
            out = pl.ds(256 * part, 256)
            acc[:, out] += dot(hbuf[:, cols], wbuf[k, part, half])

        loop(0, 2 * len(pairs), one)

    def tables():
        tri = (iota((512, 512), 0) >= iota((512, 512), 1)).astype(F32).astype(BF16)

        def split(v, parts):
            out = []
            for _ in range(parts):
                top_part = v.astype(BF16)
                out.append(top_part)
                v = v - top_part.astype(F32)
            return out

        run = sum(dot(tri, p, 1, 1) for p in split(ldv[...], 3))
        none = jnp.zeros((512, 32), F32)
        run3[...] = jnp.concatenate([p.astype(F32) for p in split(run, 3)] + [none], axis=1).astype(BF16)
        runt[...] = jnp.concatenate([run, none, none, none], axis=1).T

        first = i * 512
        begin = jnp.int32(0)
        t_col, t_row = iota((512, 128), 0), iota((8, 512), 1)
        c_col, c_row = jnp.zeros((512, 128), jnp.int32), jnp.zeros((8, 512), jnp.int32)
        c_mid, c_end = jnp.int32(0), jnp.int32(0)
        for d in range(8):
            at = begin - first
            inside = jnp.where(at >= 0, 1, 0)
            c_col += jnp.where(t_col >= at, inside, 0)
            c_row += jnp.where(t_row >= at, inside, 0)
            c_mid += jnp.where(at <= 255, inside, 0)
            c_end += jnp.where(at <= 511, inside, 0)
            begin = begin + lens[d]
        cnt[0:8, :] = c_row.astype(F32)
        col, row = c_col[:, 0:1], c_row[0:1, :]
        same = jnp.where(col == row, 1.0, 0.0)
        msk[...] = jnp.where(iota((512, 512), 0) >= iota((512, 512), 1), same, 0.0)
        seg = c_col[:, 0:32]
        ent = jnp.where(seg == 0, jnp.exp(run), 0.0)
        end = jnp.where(seg == c_end, jnp.exp(jnp.minimum(run[511:512, :] - run, 0.0)), 0.0)
        mid = jnp.where(seg == c_mid, jnp.exp(-jnp.abs(run - run[255:256, :])), 0.0)
        for ref, v in ((ent2, ent), (end2, end), (mid2, mid)):
            ref[...] = jnp.concatenate([p.astype(F32) for p in split(v, 2)] + [none, none], axis=1).astype(BF16)
        return jnp.where(c_end == 0, 1.0, 0.0)

    def spread(first_head, width, parts):
        r, c = iota((128, 256), 0), iota((128, 256), 1)
        hit = ((r & 31) == first_head + c // width) & (r < 32 * parts)
        return jnp.where(hit, 1.0, 0.0).astype(BF16)

    def scaled(c):
        cols = pl.ds(pl.multiple_of(256 * c, 256), 256)
        oh = spread(4 * c, 64, 2)
        a = (dy[:, cols].astype(F32) * dot(ent2[...], oh)).astype(BF16)
        dys[:, cols] = a
        dyst[cols, :] = a.T
        b = (x[:, cols].astype(F32) * dot(end2[...], oh)).astype(BF16)
        xs[:, cols] = b
        xst[cols, :] = b.T
        m = dot(mid2[...], oh)
        p = (x[0:256, cols].astype(F32) * m[0:256]).astype(BF16)
        q = (dy[256:512, cols].astype(F32) * m[256:512]).astype(BF16)
        xe[:, cols] = p
        de[:, cols] = q
        dg10[...] += dot(q, p, 1, 1)

    def weights(r, hp, b, e):
        rb = r[256 * b : 256 * b + 256, 128 * e : 128 * e + 128]
        rt = runt[pl.ds(2 * hp + e, 1), 256 * b : 256 * b + 256]
        return jnp.concatenate([rb, rb], axis=1) - rt

    def one_head(v, e):
        return jnp.where((iota(v.shape, 1) // 64) == e, v, jnp.zeros_like(v))

    def dgram_pair(hp):
        r = dot(run3[...], spread(2 * hp, 128, 3))
        cols = pl.ds(pl.multiple_of(128 * hp, 128), 128)
        for b in (0, 1):
            rs = slice(256 * b, 256 * b + 256)
            dyp, xp = dy[rs, cols], x[rs, cols]
            total = dgd[b]
            for e in (0, 1):
                s = dot(dyp, one_head(xp, e), 1, 1)
                total += s * jnp.exp(jnp.minimum(weights(r, hp, b, e), 0.0))
            dgd[b] = total
        tail = jnp.exp(r[504:512, :])
        dtile[hp, 0:1, :] = tail[7:8, 0:128] * whole
        dtile[hp, 1:2, :] = tail[7:8, 128:256] * whole

    def send_decays():
        drecv[i] = dtile[i]

        def one(d):
            q = lax.rem(i + d, 16)
            remote(dtile.at[q], drecv.at[i], tsend.at[4, q], trecv.at[4, i], (q, j)).start()

        loop(1, 16, one)

    def pair_rows(q):
        return pl.ds(pl.multiple_of(128 * q, 128), 128)

    def states(kind, left, cols, out, into):
        def one(d):
            q = lax.rem(i + d, 16)
            out[q] = dot(left[pair_rows(q), :], bc[:, cols]).astype(BF16)
            remote(out.at[q], into.at[i], tsend.at[kind, q], trecv.at[kind, i], (q, j)).start()

        loop(1, 16, one)
        into[i] = dot(left[pair_rows(i), :], bc[:, cols]).astype(BF16)

    def wait_in(kind, into):
        def one(d):
            k = lax.rem(i + d, 16)
            ref = into.at[pair_rows(k), :] if kind in (2, 3) else into.at[k]
            remote(ref, ref, tsend.at[kind, k], trecv.at[kind, k], (k, j)).wait_recv()

        loop(1, 16, one)

    def wait_out(kind, src):
        def one(d):
            k = lax.rem(i + d, 16)
            remote(src.at[k], src.at[k], tsend.at[kind, k], trecv.at[kind, k], (k, j)).wait_send()

        loop(1, 16, one)

    def scan(kind, into, out, back, backward):
        def one(n, state):
            k = 15 - n if backward else n
            out[k] = state.astype(BF16)
            d = drecv[k]
            d0 = jnp.concatenate([d[0:1, :], d[0:1, :]], axis=1)
            d1 = jnp.concatenate([d[1:2, :], d[1:2, :]], axis=1)
            new = into[k].astype(F32)
            return jnp.concatenate([state[0:64] * d0 + new[0:64], state[64:128] * d1 + new[64:128]], axis=0)

        lax.fori_loop(0, 16, one, jnp.zeros((128, 256), F32))

        def ship(d):
            k = lax.rem(i + d, 16)
            remote(out.at[k], back.at[pair_rows(i), :], tsend.at[kind, k], trecv.at[kind, i], (k, j)).start()

        loop(1, 16, ship)
        back[pair_rows(i), :] = out[i]

    def intra_pair(hp):
        r = dot(run3[...], spread(2 * hp, 128, 3))
        cols = pl.ds(pl.multiple_of(128 * hp, 128), 128)
        for b in (0, 1):
            rs = slice(256 * b, 256 * b + 256)
            dyp, xp = dy[rs, cols], x[rs, cols]
            ya = jnp.zeros((256, 128), F32)
            da = jnp.zeros((256, 128), F32)
            for e in (0, 1):
                diff = weights(r, hp, b, e)
                mix = (gd[b] * jnp.exp(jnp.minimum(diff, 0.0))).astype(BF16)
                ya += dot(mix, one_head(xp, e))
                mixt = (gdt[b] * jnp.exp(jnp.minimum(-diff, 0.0))).astype(BF16)
                da += dot(mixt, one_head(dyp, e))
            yacc[rs, cols] = ya
            dxacc[rs, cols] = da

    def across(c):
        cols = pl.ds(pl.multiple_of(256 * c, 256), 256)
        m = dot(mid2[...], spread(4 * c, 64, 2))
        yacc[256:512, cols] += m[256:512] * dot(g10[...], xe[:, cols])
        dxacc[0:256, cols] += m[0:256] * dot(g10t[...], de[:, cols])

    for c in loads[0:4]:
        c.wait()
    step0(0)
    acc[...] = jnp.zeros_like(acc)
    dg10[...] = jnp.zeros_like(dg10)
    dgd[...] = jnp.zeros_like(dgd)
    dtile[...] = jnp.zeros_like(dtile)
    loads[4].wait()
    whole = tables()
    loads[5].wait()
    loads[6].wait()
    step1(0)
    step0(1)
    loads[7].wait()
    mul(0, [(0, 0), (-1, 0), (1, 0)])
    fwd_b(0, (0,))
    loop(0, 4, dgram_pair)
    step3(0)
    step1(1)
    mul(0, [(0, -1), (0, 1), (2, 0)])
    mul(1, [(0, 0), (-1, 0), (1, 0)])
    fwd_b(0, (-1, 1))
    fwd_b(1, (0,))
    loop(4, 10, dgram_pair)
    fwd_b(0, (2,))
    step3(1)
    loop(0, 4, scaled)
    mul(0, [(-1, -1), (-1, 1), (1, -1), (1, 1)])
    fwd_b(1, (-1, 1))
    mul(1, [(0, -1), (0, 1), (2, 0)])
    loop(4, 8, scaled)
    last(0, (0, -1, 1))
    mul(0, [(2, -1), (2, 1), (0, 2), (-1, 2), (1, 2)])
    fwd_b(1, (2,))
    last(0, (2,))
    mul(0, [(2, 2)])
    bc[:, 0:256] = acc[:, 0:256].astype(BF16)
    states(0, xst, slice(0, 256), ssend, frecv)
    mul(1, [(-1, -1), (-1, 1), (1, -1), (1, 1), (2, -1), (2, 1)])
    loop(10, 16, dgram_pair)
    send_decays()
    last(1, (0, -1, 1))
    mul(1, [(0, 2), (-1, 2), (1, 2)])
    last(1, (2,))
    mul(1, [(2, 2)])
    bc[:, 256:512] = acc[:, 256:512].astype(BF16)
    states(1, dyst, slice(256, 512), gsend, grecv)
    dgb[0:256, 0:256] = (dgd[0] * msk[0:256, 0:256]).astype(BF16)
    dgb[256:512, 256:512] = (dgd[1] * msk[256:512, 256:512]).astype(BF16)
    dgb[256:512, 0:256] = (dg10[...] * msk[256:512, 0:256]).astype(BF16)
    dgb[0:256, 256:512] = jnp.zeros((256, 256), BF16)
    b_map, c_map = bc[:, 0:256], bc[:, 256:512]
    row = cnt[0:1, :]
    for b in (0, 1):
        rs = slice(256 * b, 256 * b + 256)
        gd[b] = dot(c_map[rs], b_map[rs], 1, 1) * msk[rs, rs]
        gdt[b] = dot(b_map[rs], c_map[rs], 1, 1) * msk[rs, rs].T
    g10[...] = (dot(c_map[256:512], b_map[0:256], 1, 1) * msk[256:512, 0:256]).astype(BF16)
    g10t[...] = (dot(b_map[0:256], c_map[256:512], 1, 1) * msk[256:512, 0:256].T).astype(BF16)
    acc[:, 0:256] = dot(dgb[...], c_map, 0, 0)
    acc[:, 256:512] = dot(dgb[...], b_map)
    loop(0, 6, intra_pair)
    wait_in(4, drecv)
    wait_in(0, frecv)
    wait_out(0, ssend)
    scan(2, frecv, ssend, sin, False)
    loop(6, 10, intra_pair)
    wait_in(1, grecv)
    wait_out(1, gsend)
    scan(3, grecv, gsend, rsum, True)
    loop(10, 16, intra_pair)
    loop(0, 8, across)
    def part_of(n):
        g = n // 4
        return 1 - lax.rem(n // 2, 2), lax.rem(2 + 3 * g + 3 * (g // 2) + 2 * (g // 3), 4), lax.rem(n, 2)

    def at_rows(part, at, size):
        return pl.ds(pl.multiple_of(256 * part + at, 128), size)

    def at_cols(half):
        return pl.ds(pl.multiple_of(256 * half, 256), 256)

    def floored(v):
        return jnp.floor(v.astype(F32) * scale + 0.5)

    def msg(n, t, src, dst, axis, sign, half):
        return remote(src, dst, rsend.at[n, t], rrecv.at[n, t], device(half, axis, sign))

    def stage0(n):
        part, da, half = part_of(n)
        k = owner(half, da, 2)
        for t, sign in ((0, 1), (1, -1)):
            src = wbuf.at[k, part, half, 128 * t : 128 * t + 128, :]
            msg(n, t, src, s1.at[n, t], "b", sign, half).start()

    def block_of(part):
        def block(k):
            cols = pl.ds(pl.multiple_of(512 * k, 512), 512)
            p = dot(dgb[256 * part : 256 * part + 256, :], hbuf[:, cols])
            top[...] = jnp.maximum(top[...], jnp.max(jnp.abs(p).reshape(32, 8, 512), axis=0))
            wbuf[k, part, 0] = p[:, 0:256].astype(BF16)
            wbuf[k, part, 1] = p[:, 256:512].astype(BF16)

        loop(0, 16, block)

    top[...] = jnp.zeros_like(top)
    for c in sent:
        c.wait_send()
    wait_in(2, sin)
    acc[:, 256:512] += dot(dys[...], sin[...])
    dgb[256:512, :] = acc[:, 256:512].T.astype(BF16)
    block_of(1)
    wait_in(3, rsum)
    loop(0, 8, lambda m: stage0(4 * (m // 2) + lax.rem(m, 2)))
    acc[:, 0:256] += dot(xs[...], rsum[...])
    dgb[0:256, :] = acc[:, 0:256].T.astype(BF16)
    block_of(0)
    loop(0, 8, lambda m: stage0(4 * (m // 2) + 2 + lax.rem(m, 2)))
    def finish_y(c):
        cols = pl.ds(pl.multiple_of(256 * c, 256), 256)
        oh = spread(4 * c, 64, 2)
        c_map, b_map = bc[:, 256:512], bc[:, 0:256]
        for t in (0, 1):
            at = pl.ds(pl.multiple_of(256 * c + 128 * t, 128), 128)
            hs = slice(128 * t, 128 * t + 128)
            carry = dot(c_map, sin[at, :], 1, 1) * dot(ent2[...], oh[:, hs])
            hbuf[:, at] = (yacc[:, at] + carry).astype(BF16)
            carry = dot(b_map, rsum[at, :], 1, 1) * dot(end2[...], oh[:, hs])
            hbuf[:, pl.ds(pl.multiple_of(2048 + 256 * c + 128 * t, 128), 128)] = (dxacc[:, at] + carry).astype(BF16)

    def ship_max(kind, count, dev):
        base = 16 * kind
        loop(1, count, lambda d: remote(
            box.at[base], box.at[base + d], msend.at[base + d], mrecv.at[base + d], dev(d)).start())

    def best_of(kind, count, dev):
        base = 16 * kind
        loop(1, count, lambda d: remote(
            box.at[base], box.at[base + d], msend.at[base + d], mrecv.at[base + d], dev(d)).wait())
        best = box[base]
        for d in range(1, count):
            best = jnp.maximum(best, box[base + d])
        return best

    along_seq = (16, lambda d: (lax.rem(i + d, 16), j))
    along_mp = (8, lambda d: (i, lax.rem(j + d, 8)))
    most = top[:, 0:128]
    for c in range(1, 4):
        most = jnp.maximum(most, top[:, 128 * c : 128 * c + 128])
    box[0] = most
    ship_max(0, *along_seq)
    loop(0, 4, finish_y)
    box[16] = best_of(0, *along_seq)
    ship_max(1, *along_mp)
    loop(4, 8, finish_y)
    best = jnp.full((8, 128), jnp.max(best_of(1, *along_mp)), F32)
    guess = jnp.ceil(jnp.log2(best)).astype(jnp.int32)
    guess = jnp.where(power_of_two(guess) < best, guess + 1, guess)
    guess = jnp.where(power_of_two(guess - 1) >= best, guess - 1, guess)
    exp_out[...] = guess.astype(F32)
    scale = jnp.max(power_of_two(20 - guess))

    def stage1(n):
        part, da, half = part_of(n)
        for t, sign in ((0, 1), (1, -1)):
            piece = wbuf.at[owner(half, da, sign), part, half]
            with_sum = slice(128 * t, 128 * t + 128)
            alone = slice(128 - 128 * t, 256 - 128 * t)
            piece[alone, :] = floored(piece[alone, :]).astype(BF16)
            own = floored(piece[with_sum, :])
            msg(n, t, s1.at[n, t], s1.at[n, t], "b", 1, half).wait_recv()
            piece[with_sum, :] = (own + floored(s1[n, t])).astype(BF16)
            msg(n, 2 + t, piece, f1.at[n, t], "b", sign, half).start()

    def total1(n):
        part, da, half = part_of(n)
        k = owner(half, da, 0)
        own = floored(wbuf[k, part, half])
        for t in (0, 1):
            msg(n, 2 + t, f1.at[n, t], f1.at[n, t], "b", 1, half).wait_recv()
        return k, part, half, own + f1[n, 0].astype(F32) + f1[n, 1].astype(F32)

    def stage2(n):
        k, part, half, total = total1(n)
        wbuf[k, part, half] = total.astype(BF16)

    def stage3(s):
        part, half = 1 - s // 2, lax.rem(s, 2)
        k = owner(half, 2, 0)
        for t, sign in ((0, 1), (1, -1)):
            src = wbuf.at[k, part, half, 128 * t : 128 * t + 128, :]
            msg(16 + s, t, src, s2.at[s, t], "a", sign, half).start()

    def stage4(s):
        part, half = 1 - s // 2, lax.rem(s, 2)
        for t, sign in ((0, 1), (1, -1)):
            piece = wbuf.at[owner(half, sign, 0), part, half]
            rs = slice(128 * t, 128 * t + 128)
            msg(16 + s, t, s2.at[s, t], s2.at[s, t], "a", 1, half).wait_recv()
            piece[rs, :] = (piece[rs, :].astype(F32) + s2[s, t].astype(F32)).astype(BF16)
            msg(16 + s, 2 + t, piece, f2.at[s, t], "a", sign, half).start()

    def stage5(n):
        _, part, half, total = total1(n)
        acc[at_rows(part, 0, 256), at_cols(half)] = total

    def stage6(s):
        part, half = 1 - s // 2, lax.rem(s, 2)
        for t in (0, 1):
            msg(16 + s, 2 + t, f2.at[s, t], f2.at[s, t], "a", 1, half).wait_recv()
        rs, cs = at_rows(part, 0, 256), at_cols(half)
        gm_out[rs, cs] = acc[rs, cs] + f2[s, 0].astype(F32) + f2[s, 1].astype(F32)

    ends = [
        pltpu.make_async_copy(hbuf.at[:, 0:2048], y_out, lsem.at[0]),
        pltpu.make_async_copy(hbuf.at[:, 2048:4096], dx_out, lsem.at[1]),
    ]
    for c in ends:
        c.start()
    loop(0, 8, stage1)
    loop(0, 4, stage2)
    loop(0, 4, stage3)
    loop(8, 12, stage1)
    loop(4, 8, stage2)
    loop(12, 16, stage1)
    loop(8, 12, stage2)
    loop(0, 4, stage4)
    loop(12, 16, stage5)
    loop(0, 4, stage6)

    for kind, src in ((2, ssend), (3, gsend), (4, dtile)):
        wait_out(kind, src)

    def left(n):
        for t in (0, 1):
            msg(n, t, s1.at[0, 0], s1.at[0, 0], "b", 1, 0).wait_send()
            msg(n, 2 + t, f1.at[0, 0], f1.at[0, 0], "b", 1, 0).wait_send()

    loop(0, 20, left)
    for c in ends:
        c.wait()


def finish(y_in, dx_in, gm_in, exp_in, y_out, dx_out, gm_out, exp_out):
    y_out[...] = y_in[...]
    dx_out[...] = dx_in[...]
    gm_out[...] = (gm_in[...] * 2.0 ** -20).T
    exp_out[...] = exp_in[0:1, 0:1]


def mixer(lengths, hidden, w, x, log_decay, dy):
    n = len(PLAN)
    vm = pltpu.VMEM
    anyw = pl.BlockSpec(memory_space=pl.ANY)
    vspec = pl.BlockSpec(memory_space=pltpu.VMEM)
    scratch = [
        vm((32, 512), F32), vm((512, 8192), BF16), vm((16, 2, 2, 256, 256), BF16), vm((512, 512), F32), vm((512, 512), BF16),
        vm((512, 2048), BF16), vm((512, 2048), BF16), vm((512, 2048), BF16), vm((512, 2048), BF16),
        vm((2048, 512), BF16), vm((2048, 512), BF16), vm((256, 2048), BF16), vm((256, 2048), BF16),
        vm((512, 2048), F32), vm((512, 2048), F32),
        vm((512, 128), BF16), vm((128, 512), F32), vm((512, 128), BF16), vm((512, 128), BF16), vm((512, 128), BF16),
        vm((8, 512), F32), vm((512, 512), F32), vm((2, 256, 256), F32), vm((256, 256), F32), vm((512, 512), BF16),
        vm((2, 256, 256), F32), vm((2, 256, 256), F32), vm((256, 256), BF16), vm((256, 256), BF16),
        vm((16, 128, 256), BF16), vm((16, 128, 256), BF16), vm((16, 128, 256), BF16), vm((16, 128, 256), BF16),
        vm((2048, 256), BF16), vm((2048, 256), BF16),
        vm((16, 8, 128), F32), vm((16, 8, 128), F32),
        vm((16, 2, 128, 256), BF16), vm((16, 2, 256, 256), BF16), vm((4, 2, 128, 256), BF16), vm((4, 2, 256, 256), BF16),
        vm((8, 512), F32), vm((32, 8, 128), F32),
        pltpu.SemaphoreType.DMA((8,)), pltpu.SemaphoreType.DMA((2, 2, n)), pltpu.SemaphoreType.DMA((2, 2, n)),
        pltpu.SemaphoreType.DMA((5, 16)), pltpu.SemaphoreType.DMA((5, 16)),
        pltpu.SemaphoreType.DMA((20, 4)), pltpu.SemaphoreType.DMA((20, 4)),
        pltpu.SemaphoreType.DMA((32,)), pltpu.SemaphoreType.DMA((32,)),
    ]
    y, dx, gm, ex = pl.pallas_call(
        kernel,
        out_shape=(
            jax.ShapeDtypeStruct((512, 2048), BF16), jax.ShapeDtypeStruct((512, 2048), BF16),
            jax.ShapeDtypeStruct((512, 512), F32), jax.ShapeDtypeStruct((8, 128), F32),
        ),
        in_specs=[pl.BlockSpec(memory_space=pltpu.SMEM), anyw, anyw, anyw, anyw, anyw],
        out_specs=(anyw, anyw, vspec, vspec),
        scratch_shapes=scratch,
        compiler_params=pltpu.CompilerParams(collective_id=0, has_side_effects=True, vmem_limit_bytes=63 * MB),
        name="mixer",
    )(lengths, log_decay.T, hidden, w, x, dy)
    y, dx, gm, ex = pl.pallas_call(
        finish,
        out_shape=(
            jax.ShapeDtypeStruct((512, 2048), BF16), jax.ShapeDtypeStruct((512, 2048), BF16),
            jax.ShapeDtypeStruct((512, 512), F32), jax.ShapeDtypeStruct((1, 1), F32),
        ),
        grid=(4,),
        in_specs=[
            pl.BlockSpec((128, 2048), lambda g: (g, 0)), pl.BlockSpec((128, 2048), lambda g: (g, 0)),
            pl.BlockSpec((512, 128), lambda g: (0, g)), pl.BlockSpec((8, 128), lambda g: (0, 0)),
        ],
        out_specs=(
            pl.BlockSpec((128, 2048), lambda g: (g, 0)), pl.BlockSpec((128, 2048), lambda g: (g, 0)),
            pl.BlockSpec((128, 512), lambda g: (g, 0)), pl.BlockSpec((1, 1), lambda g: (0, 0)),
        ),
        name="finish",
    )(y, dx, gm, ex)
    return y, dx, gm, ex.reshape(())


def solution(mesh):
    in_specs = (P(), P("seq", None), P("seq", "mp"), P("seq", "mp"), P("seq", "mp"), P("seq", "mp"))
    out_specs = (P("seq", "mp"), P("seq", "mp"), P("seq", "mp"), P())
    return jax.shard_map(mixer, mesh=mesh, in_specs=in_specs, out_specs=out_specs, check_vma=False)
```

time: 190 us -> 176 us (0.926)
  local copies, waits for them, and re-layouts: 9.11 us -> 0 us
  Pallas kernels: 180 us -> 174 us
    pallas_call x1, Pallas kernels: 180 us -> 169 us  [mixer(): pl.pallas_call(kernel, out_shape=(jax.ShapeDtypeStruct((512, 2048), BF16)...]
    unnamed x8 -> x0, local copies, waits for them, and re-layouts: 7.91 us -> none
    pallas_call x0 -> x1, Pallas kernels: none -> 5.31 us  [mixer(): pl.pallas_call(finish, out_shape=(jax.ShapeDtypeStruct((512, 2048), BF16)...]
where the time goes in v3:
time: 176 us; the launch traced here: 175 us
  Pallas kernels  174 us (99%)
    pallas_call x1, Pallas kernels, mixer(): pl.pallas_call(kernel, out_shape=(jax.ShapeDtypeStruct((512, 2048), BF16)...  169 us
    pallas_call x1, Pallas kernels, mixer(): pl.pallas_call(finish, out_shape=(jax.ShapeDtypeStruct((512, 2048), BF16)...  5.31 us

profile of v3, /device:TPU:0, one launch (start us, length us, event | category | flops | bytes accessed | tf_op | source)
XLA Modules:
  0.0 175.0 jit_solution(2210082901030314233)
XLA Ops:
  0.6 169.0 %mixer.1 = (bf16[512,2048]{1,0:T(8,128)(2,1)}, bf16[512,2048]{1,0:T(8,128)(2,1)}, f32[512,512]{1,0:T(8,128)}, f32[8,128]{1,0:T(8,128)}) custom-call(s32[8]{0:T(128)} %lens.1, f32[32,512]{1,0:T(8,128)} %bitcast.2, bf16[512,8192]{1,0:T(8,128)(2,1)} %hid.1, bf16[512,512]{1,0:T(8,128)(2,1)} %w.1, bf16[512,2048]{1,0:T(8,128)(2,1)} %xin.1, bf16[512,2048]{1,0:T(8,128)(2,1)} %dyin.1), custom_call_target="tpu_custom_call" | custom-call | tf_op jit(solution)/shard_map/mixer/pallas_call | solution.py:614
  169.7 5.3 %finish.1 = (bf16[512,2048]{1,0:T(8,128)(2,1)}, bf16[512,2048]{1,0:T(8,128)(2,1)}, f32[512,512]{1,0:T(8,128)}, f32[1,1]{1,0:T(1,128)}) custom-call(bf16[512,2048]{1,0:T(8,128)(2,1)} %get-tuple-element.12.y_in, bf16[512,2048]{1,0:T(8,128)(2,1)} %get-tuple-element.13.dx_in, f32[512,512]{1,0:T(8,128)} %get-tuple-element.14.gm_in, f32[8,128]{1,0:T(8,128)} %get-tuple-element.15.exp_in), custom_call_target="tpu_custom_call" | custom-call | tf_op jit(solution)/shard_map/finish/pallas_call | solution.py:626

commit v4 on v3

--- a/solution.py
+++ b/solution.py
@@ -41,6 +41,8 @@
 
 
 PLAN = gather_plan()
+
+NEAR = [(0, 1), (1, 0), (0, 3), (3, 0), (1, 1), (3, 3), (1, 3), (3, 1), (0, 2), (2, 0), (1, 2), (2, 1), (3, 2), (2, 3), (2, 2)]
 
 
 def power_of_two(n):
@@ -272,14 +274,13 @@
     def pair_rows(q):
         return pl.ds(pl.multiple_of(128 * q, 128), 128)
 
-    def states(kind, left, cols, out, into):
-        def one(d):
-            q = lax.rem(i + d, 16)
+    def states(kind, left, cols, out, into, peers):
+        for dx, dyy in peers:
+            q = owner(1, dx, dyy)
             out[q] = dot(left[pair_rows(q), :], bc[:, cols]).astype(BF16)
             remote(out.at[q], into.at[i], tsend.at[kind, q], trecv.at[kind, i], (q, j)).start()
-
-        loop(1, 16, one)
-        into[i] = dot(left[pair_rows(i), :], bc[:, cols]).astype(BF16)
+        if peers[0] == NEAR[0]:
+            into[i] = dot(left[pair_rows(i), :], bc[:, cols]).astype(BF16)
 
     def wait_in(kind, into):
         def one(d):
@@ -308,11 +309,9 @@
 
         lax.fori_loop(0, 16, one, jnp.zeros((128, 256), F32))
 
-        def ship(d):
-            k = lax.rem(i + d, 16)
+        for dx, dyy in NEAR:
+            k = owner(1, dx, dyy)
             remote(out.at[k], back.at[pair_rows(i), :], tsend.at[kind, k], trecv.at[kind, i], (k, j)).start()
-
-        loop(1, 16, ship)
         back[pair_rows(i), :] = out[i]
 
     def intra_pair(hp):
@@ -375,7 +374,7 @@
     last(0, (2,))
     mul(0, [(2, 2)])
     bc[:, 0:256] = acc[:, 0:256].astype(BF16)
-    states(0, xst, slice(0, 256), ssend, frecv)
+    states(0, xst, slice(0, 256), ssend, frecv, NEAR)
     mul(1, [(-1, -1), (-1, 1), (1, -1), (1, 1), (2, -1), (2, 1)])
     loop(10, 16, dgram_pair)
     send_decays()
@@ -384,7 +383,7 @@
     last(1, (2,))
     mul(1, [(2, 2)])
     bc[:, 256:512] = acc[:, 256:512].astype(BF16)
-    states(1, dyst, slice(256, 512), gsend, grecv)
+    states(1, dyst, slice(256, 512), gsend, grecv, NEAR[0:8])
     dgb[0:256, 0:256] = (dgd[0] * msk[0:256, 0:256]).astype(BF16)
     dgb[256:512, 256:512] = (dgd[1] * msk[256:512, 256:512]).astype(BF16)
     dgb[256:512, 0:256] = (dg10[...] * msk[256:512, 0:256]).astype(BF16)
@@ -399,17 +398,16 @@
     g10t[...] = (dot(b_map[0:256], c_map[256:512], 1, 1) * msk[256:512, 0:256].T).astype(BF16)
     acc[:, 0:256] = dot(dgb[...], c_map, 0, 0)
     acc[:, 256:512] = dot(dgb[...], b_map)
-    loop(0, 6, intra_pair)
     wait_in(4, drecv)
     wait_in(0, frecv)
     wait_out(0, ssend)
     scan(2, frecv, ssend, sin, False)
-    loop(6, 10, intra_pair)
+    states(1, dyst, slice(256, 512), gsend, grecv, NEAR[8:15])
+    loop(0, 6, intra_pair)
     wait_in(1, grecv)
     wait_out(1, gsend)
     scan(3, grecv, gsend, rsum, True)
-    loop(10, 16, intra_pair)
-    loop(0, 8, across)
+    loop(6, 10, intra_pair)
     def part_of(n):
         g = n // 4
         return 1 - lax.rem(n // 2, 2), lax.rem(2 + 3 * g + 3 * (g // 2) + 2 * (g // 3), 4), lax.rem(n, 2)
@@ -455,7 +453,6 @@
     acc[:, 0:256] += dot(xs[...], rsum[...])
     dgb[0:256, :] = acc[:, 0:256].T.astype(BF16)
     block_of(0)
-    loop(0, 8, lambda m: stage0(4 * (m // 2) + 2 + lax.rem(m, 2)))
     def finish_y(c):
         cols = pl.ds(pl.multiple_of(256 * c, 256), 256)
         oh = spread(4 * c, 64, 2)
@@ -489,10 +486,11 @@
         most = jnp.maximum(most, top[:, 128 * c : 128 * c + 128])
     box[0] = most
     ship_max(0, *along_seq)
-    loop(0, 4, finish_y)
+    loop(0, 8, lambda m: stage0(4 * (m // 2) + 2 + lax.rem(m, 2)))
+    loop(10, 13, intra_pair)
     box[16] = best_of(0, *along_seq)
     ship_max(1, *along_mp)
-    loop(4, 8, finish_y)
+    loop(13, 16, intra_pair)
     best = jnp.full((8, 128), jnp.max(best_of(1, *along_mp)), F32)
     guess = jnp.ceil(jnp.log2(best)).astype(jnp.int32)
     guess = jnp.where(power_of_two(guess) < best, guess + 1, guess)
@@ -551,18 +549,21 @@
         rs, cs = at_rows(part, 0, 256), at_cols(half)
         gm_out[rs, cs] = acc[rs, cs] + f2[s, 0].astype(F32) + f2[s, 1].astype(F32)
 
+    loop(0, 8, stage1)
+    loop(0, 8, across)
+    loop(0, 4, stage2)
+    loop(0, 4, stage3)
+    loop(8, 12, stage1)
+    loop(0, 4, finish_y)
+    loop(4, 8, stage2)
+    loop(12, 16, stage1)
+    loop(4, 8, finish_y)
     ends = [
         pltpu.make_async_copy(hbuf.at[:, 0:2048], y_out, lsem.at[0]),
         pltpu.make_async_copy(hbuf.at[:, 2048:4096], dx_out, lsem.at[1]),
     ]
     for c in ends:
         c.start()
-    loop(0, 8, stage1)
-    loop(0, 4, stage2)
-    loop(0, 4, stage3)
-    loop(8, 12, stage1)
-    loop(4, 8, stage2)
-    loop(12, 16, stage1)
     loop(8, 12, stage2)
     loop(0, 4, stage4)
     loop(12, 16, stage5)
@@ -581,11 +582,32 @@
         c.wait()
 
 
-def finish(y_in, dx_in, gm_in, exp_in, y_out, dx_out, gm_out, exp_out):
-    y_out[...] = y_in[...]
-    dx_out[...] = dx_in[...]
-    gm_out[...] = (gm_in[...] * 2.0 ** -20).T
+def finish(y_in, dx_in, gm_in, exp_in, y_out, dx_out, gm_out, exp_out, buf, gbuf, gout, sem, out_sem):
+    pieces, size = 2, 256
+    moves = []
+    for a, (src, dst) in enumerate(((y_in, y_out), (dx_in, dx_out))):
+        for p in range(pieces):
+            rows = pl.ds(size * p, size)
+            n = a * pieces + p
+            moves.append((
+                pltpu.make_async_copy(src.at[rows, :], buf.at[a, rows, :], sem.at[n]),
+                pltpu.make_async_copy(buf.at[a, rows, :], dst.at[rows, :], out_sem.at[n]),
+            ))
+    g_in = pltpu.make_async_copy(gm_in, gbuf, sem.at[2 * pieces])
+    g_out = pltpu.make_async_copy(gout, gm_out, out_sem.at[2 * pieces])
+    g_in.start()
+    for load, _ in moves:
+        load.start()
     exp_out[...] = exp_in[0:1, 0:1]
+    g_in.wait()
+    gout[...] = (gbuf[...] * 2.0 ** -20).T
+    g_out.start()
+    for load, store in moves:
+        load.wait()
+        store.start()
+    for _, store in moves:
+        store.wait()
+    g_out.wait()
 
 
 def mixer(lengths, hidden, w, x, log_decay, dy):
@@ -629,15 +651,13 @@
             jax.ShapeDtypeStruct((512, 2048), BF16), jax.ShapeDtypeStruct((512, 2048), BF16),
             jax.ShapeDtypeStruct((512, 512), F32), jax.ShapeDtypeStruct((1, 1), F32),
         ),
-        grid=(4,),
-        in_specs=[
-            pl.BlockSpec((128, 2048), lambda g: (g, 0)), pl.BlockSpec((128, 2048), lambda g: (g, 0)),
-            pl.BlockSpec((512, 128), lambda g: (0, g)), pl.BlockSpec((8, 128), lambda g: (0, 0)),
+        in_specs=[anyw, anyw, anyw, vspec],
+        out_specs=(anyw, anyw, anyw, vspec),
+        scratch_shapes=[
+            vm((2, 512, 2048), BF16), vm((512, 512), F32), vm((512, 512), F32),
+            pltpu.SemaphoreType.DMA((5,)), pltpu.SemaphoreType.DMA((5,)),
         ],
-        out_specs=(
-            pl.BlockSpec((128, 2048), lambda g: (g, 0)), pl.BlockSpec((128, 2048), lambda g: (g, 0)),
-            pl.BlockSpec((128, 512), lambda g: (g, 0)), pl.BlockSpec((1, 1), lambda g: (0, 0)),
-        ),
+        compiler_params=pltpu.CompilerParams(vmem_limit_bytes=62 * MB),
         name="finish",
     )(y, dx, gm, ex)
     return y, dx, gm, ex.reshape(())

time: 176 us -> 165 us (0.938)
  Pallas kernels: 174 us -> 164 us
    pallas_call x1, Pallas kernels: 169 us -> 158 us  [mixer(): pl.pallas_call(kernel, out_shape=(jax.ShapeDtypeStruct((512, 2048), BF16)...]
where the time goes in v4:
time: 165 us; the launch traced here: 164 us
  Pallas kernels  164 us (99%)
    pallas_call x1, Pallas kernels, mixer(): pl.pallas_call(kernel, out_shape=(jax.ShapeDtypeStruct((512, 2048), BF16)...  158 us
    pallas_call x1, Pallas kernels, mixer(): pl.pallas_call(finish, out_shape=(jax.ShapeDtypeStruct((512, 2048), BF16)...  5.19 us

profile of v4, /device:TPU:0, one launch (start us, length us, event | category | flops | bytes accessed | tf_op | source)
XLA Modules:
  0.0 164.4 jit_solution(10560152893237506961)
XLA Ops:
  0.6 158.4 %mixer.1 = (bf16[512,2048]{1,0:T(8,128)(2,1)}, bf16[512,2048]{1,0:T(8,128)(2,1)}, f32[512,512]{1,0:T(8,128)}, f32[8,128]{1,0:T(8,128)}) custom-call(s32[8]{0:T(128)} %lens.1, f32[32,512]{1,0:T(8,128)} %bitcast.2, bf16[512,8192]{1,0:T(8,128)(2,1)} %hid.1, bf16[512,512]{1,0:T(8,128)(2,1)} %w.1, bf16[512,2048]{1,0:T(8,128)(2,1)} %xin.1, bf16[512,2048]{1,0:T(8,128)(2,1)} %dyin.1), custom_call_target="tpu_custom_call" | custom-call | tf_op jit(solution)/shard_map/mixer/pallas_call | solution.py:636
  159.0 5.2 %finish.1 = (bf16[512,2048]{1,0:T(8,128)(2,1)}, bf16[512,2048]{1,0:T(8,128)(2,1)}, f32[512,512]{1,0:T(8,128)}, f32[1,1]{1,0:T(1,128)}) custom-call(bf16[512,2048]{1,0:T(8,128)(2,1)} %get-tuple-element.12.y_in, bf16[512,2048]{1,0:T(8,128)(2,1)} %get-tuple-element.13.dx_in, f32[512,512]{1,0:T(8,128)} %get-tuple-element.14.gm_in, f32[8,128]{1,0:T(8,128)} %get-tuple-element.15.exp_in), custom_call_target="tpu_custom_call" | custom-call | tf_op jit(solution)/shard_map/finish/pallas_call | solution.py:648

commit v5 on v4

--- a/solution.py
+++ b/solution.py
@@ -407,7 +407,7 @@
     wait_in(1, grecv)
     wait_out(1, gsend)
     scan(3, grecv, gsend, rsum, True)
-    loop(6, 10, intra_pair)
+    loop(6, 9, intra_pair)
     def part_of(n):
         g = n // 4
         return 1 - lax.rem(n // 2, 2), lax.rem(2 + 3 * g + 3 * (g // 2) + 2 * (g // 3), 4), lax.rem(n, 2)
@@ -433,8 +433,7 @@
 
     def block_of(part):
         def block(k):
-            cols = pl.ds(pl.multiple_of(512 * k, 512), 512)
-            p = dot(dgb[256 * part : 256 * part + 256, :], hbuf[:, cols])
+            p = dot(dgb[256 * part : 256 * part + 256, :], hbuf[:, pl.ds(pl.multiple_of(512 * k, 512), 512)])
             top[...] = jnp.maximum(top[...], jnp.max(jnp.abs(p).reshape(32, 8, 512), axis=0))
             wbuf[k, part, 0] = p[:, 0:256].astype(BF16)
             wbuf[k, part, 1] = p[:, 256:512].astype(BF16)
@@ -448,8 +447,8 @@
     acc[:, 256:512] += dot(dys[...], sin[...])
     dgb[256:512, :] = acc[:, 256:512].T.astype(BF16)
     block_of(1)
+    loop(0, 8, lambda m: stage0(4 * (m // 2) + lax.rem(m, 2)))
     wait_in(3, rsum)
-    loop(0, 8, lambda m: stage0(4 * (m // 2) + lax.rem(m, 2)))
     acc[:, 0:256] += dot(xs[...], rsum[...])
     dgb[0:256, :] = acc[:, 0:256].T.astype(BF16)
     block_of(0)
@@ -465,33 +464,33 @@
             carry = dot(b_map, rsum[at, :], 1, 1) * dot(end2[...], oh[:, hs])
             hbuf[:, pl.ds(pl.multiple_of(2048 + 256 * c + 128 * t, 128), 128)] = (dxacc[:, at] + carry).astype(BF16)
 
-    def ship_max(kind, count, dev):
-        base = 16 * kind
-        loop(1, count, lambda d: remote(
-            box.at[base], box.at[base + d], msend.at[base + d], mrecv.at[base + d], dev(d)).start())
-
-    def best_of(kind, count, dev):
-        base = 16 * kind
-        loop(1, count, lambda d: remote(
-            box.at[base], box.at[base + d], msend.at[base + d], mrecv.at[base + d], dev(d)).wait())
-        best = box[base]
-        for d in range(1, count):
-            best = jnp.maximum(best, box[base + d])
+    def ship_max(kind, peers):
+        for n, dev in enumerate(peers):
+            remote(box.at[17 * kind], box.at[17 * kind + 1 + n], msend.at[kind], mrecv.at[kind], dev).start()
+
+    def best_of(kind, peers):
+        every = box.at[pl.ds(17 * kind + 1, len(peers))]
+        remote(every, every, msend.at[kind], mrecv.at[kind], peers[0]).wait()
+        best = box[17 * kind]
+        for n in range(len(peers)):
+            best = jnp.maximum(best, box[17 * kind + 1 + n])
         return best
 
-    along_seq = (16, lambda d: (lax.rem(i + d, 16), j))
-    along_mp = (8, lambda d: (i, lax.rem(j + d, 8)))
+    along_seq = [(owner(1, dx, dyy), j) for dx, dyy in NEAR[::-1]]
+    along_mp = [(i, lax.rem(j + d, 8)) for d in (4, 3, 5, 2, 6, 1, 7)]
     most = top[:, 0:128]
     for c in range(1, 4):
         most = jnp.maximum(most, top[:, 128 * c : 128 * c + 128])
     box[0] = most
-    ship_max(0, *along_seq)
+    ship_max(0, along_seq)
+    loop(9, 13, intra_pair)
+    box[17] = best_of(0, along_seq)
+    ship_max(1, along_mp)
     loop(0, 8, lambda m: stage0(4 * (m // 2) + 2 + lax.rem(m, 2)))
-    loop(10, 13, intra_pair)
-    box[16] = best_of(0, *along_seq)
-    ship_max(1, *along_mp)
     loop(13, 16, intra_pair)
-    best = jnp.full((8, 128), jnp.max(best_of(1, *along_mp)), F32)
+    for kind, src in ((2, ssend), (3, gsend), (4, dtile)):
+        wait_out(kind, src)
+    best = jnp.full((8, 128), jnp.max(best_of(1, along_mp)), F32)
     guess = jnp.ceil(jnp.log2(best)).astype(jnp.int32)
     guess = jnp.where(power_of_two(guess) < best, guess + 1, guess)
     guess = jnp.where(power_of_two(guess - 1) >= best, guess - 1, guess)
@@ -567,17 +566,14 @@
     loop(8, 12, stage2)
     loop(0, 4, stage4)
     loop(12, 16, stage5)
-    loop(0, 4, stage6)
-
-    for kind, src in ((2, ssend), (3, gsend), (4, dtile)):
-        wait_out(kind, src)
-
     def left(n):
         for t in (0, 1):
             msg(n, t, s1.at[0, 0], s1.at[0, 0], "b", 1, 0).wait_send()
             msg(n, 2 + t, f1.at[0, 0], f1.at[0, 0], "b", 1, 0).wait_send()
 
-    loop(0, 20, left)
+    loop(0, 16, left)
+    loop(0, 4, stage6)
+    loop(16, 20, left)
     for c in ends:
         c.wait()
 
@@ -631,7 +627,7 @@
         pltpu.SemaphoreType.DMA((8,)), pltpu.SemaphoreType.DMA((2, 2, n)), pltpu.SemaphoreType.DMA((2, 2, n)),
         pltpu.SemaphoreType.DMA((5, 16)), pltpu.SemaphoreType.DMA((5, 16)),
         pltpu.SemaphoreType.DMA((20, 4)), pltpu.SemaphoreType.DMA((20, 4)),
-        pltpu.SemaphoreType.DMA((32,)), pltpu.SemaphoreType.DMA((32,)),
+        pltpu.SemaphoreType.DMA((2,)), pltpu.SemaphoreType.DMA((2,)),
     ]
     y, dx, gm, ex = pl.pallas_call(
         kernel,

time: 165 us -> 164 us (level)
  no operation moved by 1% of the time
where the time goes in v5:
time: 164 us
  Pallas kernels  163 us (99%)
    pallas_call x1, Pallas kernels, mixer(): pl.pallas_call(kernel, out_shape=(jax.ShapeDtypeStruct((512, 2048), BF16)...  158 us
    pallas_call x1, Pallas kernels, mixer(): pl.pallas_call(finish, out_shape=(jax.ShapeDtypeStruct((512, 2048), BF16)...  5.19 us

profile of v5, /device:TPU:0, one launch (start us, length us, event | category | flops | bytes accessed | tf_op | source)
XLA Modules:
  0.0 163.7 jit_solution(10186060738249335089)
XLA Ops:
  0.6 157.7 %mixer.1 = (bf16[512,2048]{1,0:T(8,128)(2,1)}, bf16[512,2048]{1,0:T(8,128)(2,1)}, f32[512,512]{1,0:T(8,128)}, f32[8,128]{1,0:T(8,128)}) custom-call(s32[8]{0:T(128)} %lens.1, f32[32,512]{1,0:T(8,128)} %bitcast.2, bf16[512,8192]{1,0:T(8,128)(2,1)} %hid.1, bf16[512,512]{1,0:T(8,128)(2,1)} %w.1, bf16[512,2048]{1,0:T(8,128)(2,1)} %xin.1, bf16[512,2048]{1,0:T(8,128)(2,1)} %dyin.1), custom_call_target="tpu_custom_call" | custom-call | tf_op jit(solution)/shard_map/mixer/pallas_call | solution.py:632
  158.4 5.2 %finish.1 = (bf16[512,2048]{1,0:T(8,128)(2,1)}, bf16[512,2048]{1,0:T(8,128)(2,1)}, f32[512,512]{1,0:T(8,128)}, f32[1,1]{1,0:T(1,128)}) custom-call(bf16[512,2048]{1,0:T(8,128)(2,1)} %get-tuple-element.12.y_in, bf16[512,2048]{1,0:T(8,128)(2,1)} %get-tuple-element.13.dx_in, f32[512,512]{1,0:T(8,128)} %get-tuple-element.14.gm_in, f32[8,128]{1,0:T(8,128)} %get-tuple-element.15.exp_in), custom_call_target="tpu_custom_call" | custom-call | tf_op jit(solution)/shard_map/finish/pallas_call | solution.py:644
